TPU v7x, 32 devices: a whole 2x2x4 slice. The times are simulated.
32 devices in a mesh: slab: 8 (over y, x, core), sub: 4 (over z).
Axes of the slice: x: 2, y: 2, z: 4, core: 2. Of those that a mesh axis runs over, the one named last changes fastest.
Arguments:
- density: float32 [2, 32, 16, 2, 296], P(None, 'slab', 'sub'), may hold values from -6 to 6
- occupied: int32 [32, 16, 2], P('slab', 'sub'), may hold values 0 or 1
- kernels: float32 [2, 316, 4096], P(None, None, ('slab', 'sub')), may hold values from -6 to 6
Outputs:
- check_potential: float32 [2, 32, 16, 2, 296], P(None, 'slab', 'sub')
All inputs are finite; a program needn't handle non-finite values. No bound on the sum of `occupied` on one device may be relied on, other than what follows from the above.
Results may differ from a plain program's by a relative error of at most 0.000071.
Values sent between devices are 32-bit elements; how exact they have to be, the bound alone decides.
No kernel may reach another device: no remote copies, remote signals or barrier semaphores. Data moves between devices by JAX's collectives and lax.ppermute only.
A program may use at most 128 MiB of HBM per device.

v0:
```python
import functools
import math

import jax
import jax.numpy as jnp
import numpy as np
from jax import lax
from jax.experimental import pallas as pl
from jax.experimental.pallas import tpu as pltpu
from jax.sharding import PartitionSpec as P

P_SIZE = 8
LANES = 128
COLUMNS = 5
VMEM_BYTES = 56 * 1024 * 1024
NEIGHBOURS = [(ex, ey) for ex in (-1, 0, 1) for ey in (-1, 0, 1) if (ex, ey) != (0, 0)]


def surface_points(edge_count):
    rows_found = []
    for first in range(edge_count):
        for second in range(edge_count):
            for third in range(edge_count):
                if min(first, second, third) == 0 or max(first, second, third) == edge_count - 1:
                    rows_found.append((first, second, third))
    return np.array(rows_found, dtype=np.int32).T


def offset_slots():
    slots = {}
    for step_x in range(-3, 4):
        for step_y in range(-3, 4):
            for step_z in range(-3, 4):
                if max(abs(step_x), abs(step_y), abs(step_z)) > 1:
                    slots[step_x, step_y, step_z] = len(slots)
    return slots


def column_groups():
    slots = offset_slots()
    return {key[:2]: slot for key, slot in slots.items() if key[2] == -1}


GROUPS = column_groups()
GROUP_ROW = {key: 3 * place for place, key in enumerate(GROUPS)}
KEPT = 3 * len(GROUPS)
KEPT_PADDED = 128


def expansion():
    weights = ((1, -1, 0), (0, -1, 1), (0, 1, 0))
    found = np.zeros((27 * 8, KEPT_PADDED), np.float32)
    for comp in range(27):
        cx, cy, cz = comp // 9, comp // 3 % 3, comp % 3
        for place, (ex, ey) in enumerate(NEIGHBOURS):
            for ax in range(3):
                for ay in range(3):
                    row = GROUP_ROW.get((2 * ex + ax - 1, 2 * ey + ay - 1))
                    if row is not None:
                        for az in range(3):
                            found[comp * 8 + place, row + az] += weights[cx][ax] * weights[cy][ay] * weights[cz][az]
    return found


def compact_body(kernel_ref, out_ref, held, sem):
    copy = pltpu.make_async_copy(kernel_ref, held, sem)
    copy.start()
    copy.wait()
    for key, slot in GROUPS.items():
        row = 2 * GROUP_ROW[key]
        out_ref[row:row + 6, :] = held[2 * slot:2 * slot + 6, :]


def compact_kernels(kernels):
    rows, width = kernels.shape[1:]
    return pl.pallas_call(
        compact_body,
        in_specs=[pl.BlockSpec(memory_space=pl.ANY)],
        out_specs=pl.BlockSpec(memory_space=pltpu.VMEM),
        out_shape=jax.ShapeDtypeStruct((2 * KEPT, width), jnp.float32),
        scratch_shapes=[pltpu.VMEM((2 * rows, width), jnp.float32), pltpu.SemaphoreType.DMA],
        name="compact",
    )(kernels.transpose(1, 0, 2).reshape(2 * rows, width))


def row_of(x, y, z):
    return (y // 2) * 16 + x * 4 + z * 2 + y % 2


def layer_start(x):
    return 64 + 28 * (x - 1)


def pack_body(occupied_ref, density_ref, out_ref, rows_re, rows_im):
    for x in range(4):
        for y in range(4):
            for z in range(2):
                keep = occupied_ref[x, z:z + 1, y:y + 1] > 0
                row = row_of(x, y, z)
                for part, rows in enumerate((rows_re, rows_im)):
                    values = density_ref[part, x, y, z:z + 1, :]
                    rows[row:row + 1, :] = jnp.where(keep, values, 0.0)
    parts = (rows_re[...], rows_im[...])
    gap = jnp.zeros((32, 4), jnp.float32)
    columns = [
        [part[:, 0:64] for part in parts],
        [part[:, 232:296] for part in parts],
    ]
    for x in (1, 3, 5):
        pieces = []
        for part in parts:
            for layer in (x, x + 1):
                at = layer_start(layer)
                pieces += [part[:, at:at + 28], gap]
        columns.append(pieces)
    for place, pieces in enumerate(columns):
        out_ref[:, place * LANES:(place + 1) * LANES] = jnp.concatenate(pieces, axis=1)


def pack(occupied, density):
    width = density.shape[-1]
    return pl.pallas_call(
        pack_body,
        in_specs=[pl.BlockSpec(memory_space=pltpu.VMEM), pl.BlockSpec(memory_space=pltpu.VMEM)],
        out_specs=pl.BlockSpec(memory_space=pltpu.VMEM),
        out_shape=jax.ShapeDtypeStruct((32, COLUMNS * LANES), jnp.float32),
        scratch_shapes=[pltpu.VMEM((32, width), jnp.float32)] * 2,
        name="pack",
    )(occupied.transpose(0, 2, 1), density)


def unpack_body(occupied_ref, p0, p1, p2, p3, out_ref, rows_re, rows_im):
    values = (p0[...] + p1[...]) + (p2[...] + p3[...])
    for part, rows in enumerate((rows_re, rows_im)):
        base = 64 * part
        pieces = [values[:, base:base + 64]]
        for layer in range(6):
            at = (2 + layer // 2) * LANES + base + 32 * (layer % 2)
            pieces.append(values[:, at:at + 28])
        pieces.append(values[:, LANES + base:LANES + base + 64])
        rows[...] = jnp.concatenate(pieces, axis=1)
    for x in range(4):
        for y in range(4):
            for z in range(2):
                keep = occupied_ref[x, z:z + 1, y:y + 1] > 0
                row = row_of(x, y, z)
                for part, rows in enumerate((rows_re, rows_im)):
                    out_ref[part, x, y, z:z + 1, :] = jnp.where(keep, rows[row:row + 1, :], 0.0)


def unpack(occupied, parts, shape):
    in_vmem = pl.BlockSpec(memory_space=pltpu.VMEM)
    return pl.pallas_call(
        unpack_body,
        in_specs=[pl.BlockSpec(memory_space=pltpu.VMEM)] + [in_vmem] * 4,
        out_specs=in_vmem,
        out_shape=jax.ShapeDtypeStruct(shape, jnp.float32),
        scratch_shapes=[pltpu.VMEM((32, shape[-1]), jnp.float32)] * 2,
        name="unpack",
    )(occupied.transpose(0, 2, 1), *parts)


def split_bf16(values):
    high = values.astype(jnp.bfloat16)
    low = (values - high.astype(jnp.float32)).astype(jnp.bfloat16)
    return high, low


def translate_body(
    sub_count, freq_part,
    c0, c1, c2, c3, inner_ref, outer_ref, factor_ref, matrix_ref, table_ref, *refs,
):
    block_count = len(refs) - 4 - 14
    block_refs, (o0, o1, o2, o3) = refs[:block_count], refs[block_count:block_count + 4]
    (
        rows, rolled, layers, spectra, comps, sums, split_sums, moved, total, tables, raw, pieces_in, kernel_ref, sems,
    ) = refs[block_count + 4:]
    slab, sub = lax.axis_index("slab"), lax.axis_index("sub")
    core = lax.rem(slab, 2)
    half_blocks = block_count // 2
    piece_count = LANES // freq_part
    class_count = tables.shape[0] // piece_count
    class_blocks = block_count // class_count
    plane = 4 * P_SIZE * P_SIZE

    variant = lax.div(lax.rem(freq_part * sub, plane), LANES) if table_ref.shape[0] > 1 else 0
    copies = [pltpu.make_async_copy(table_ref.at[variant], tables, sems.at[block_count])]
    for block, ref in enumerate(block_refs):
        copies.append(pltpu.make_async_copy(ref, raw.at[block], sems.at[block]))
    for copy in copies:
        copy.start()

    for k, chunk in enumerate((c0, c1, c2, c3)):
        source = sub ^ k
        for half in range(2):
            base = pl.multiple_of((2 * source + half) * 32, 32)
            rows[pl.ds(base + 8, 16), :] = chunk[half * 16:half * 16 + 16, :]
            at = k * 16 + half * 8
            rows[pl.ds(pl.multiple_of(base + 24 * (1 - core), 8), 8), :] = inner_ref[at:at + 8, :]
            rows[pl.ds(pl.multiple_of(base + 24 * core, 8), 8), :] = outer_ref[at:at + 8, :]
    for place in range(1, COLUMNS):
        lanes = slice(place * LANES, (place + 1) * LANES)
        for at in range(0, 256, 32):
            rolled[at:at + 32, lanes] = pltpu.roll(rows[at:at + 32, lanes], 64, 1)
    edge = jnp.zeros((54, LANES), jnp.float32)
    for parent in range(4):
        for place in (0, 9):
            at = (parent * 10 + place) * 54
            comps[at:at + 54, :] = edge
    total[...] = jnp.zeros_like(total)

    def split_store(ref, at, place, values):
        high, low = split_bf16(values)
        for third, piece in enumerate((high, low, high)):
            lanes = third * 256 + place * LANES
            ref[pl.ds(at, 16), lanes:lanes + LANES] = piece

    def factors(block, piece):
        odd = (block >= half_blocks).astype(jnp.int32)
        owner = slab ^ (2 * ((block - half_blocks * odd) * piece_count + piece) + odd)
        freq_x = lax.div(freq_part * (sub_count * owner + sub), plane)
        return [factor_ref[freq_x, row:row + 1, :] for row in range(8)]

    pieces_in[...] = jnp.zeros_like(pieces_in)

    for group in range(class_count):
        for piece in range(piece_count):

            def transform_x(index, _):
                factor = factors(group * class_blocks + index, piece)
                for at in range(0, 256, 16):
                    def column(ref, place):
                        return ref[at:at + 16, place * LANES:(place + 1) * LANES]

                    full = column(rows, 0) + (factor[0] * column(rows, 1) + factor[1] * column(rolled, 1))
                    ring = None
                    for pair in range(3):
                        term = (
                            factor[2 + 2 * pair] * column(rows, 2 + pair)
                            + factor[3 + 2 * pair] * column(rolled, 2 + pair)
                        )
                        ring = term if ring is None else ring + term
                    target = pl.multiple_of(index * 256 + at, 16)
                    split_store(layers, target, 0, full)
                    split_store(layers, target, 1, ring)
                return 0

            lax.fori_loop(0, class_blocks, transform_x, 0)
            if group == 0 and piece == 0:
                copies[0].wait()
            found = jnp.dot(layers[...], tables[group * piece_count + piece, 0], preferred_element_type=jnp.float32)
            span = slice(group * class_blocks * 256, (group + 1) * class_blocks * 256)
            for part in range(2):
                values = found[:, part * LANES:(part + 1) * LANES]
                if piece > 0:
                    values = values + spectra[part, span, :]
                spectra[part, span, :] = values

    for copy in copies[1:]:
        copy.wait()

    def expand(block, _):
        for part in range(2):
            left = raw[block, pl.ds(part, KEPT, stride=2), :]
            lanes = slice(part * LANES, (part + 1) * LANES)
            for turn in range(3):
                piece = left.astype(jnp.bfloat16)
                left = left - piece.astype(jnp.float32)
                pieces_in[turn * KEPT_PADDED:turn * KEPT_PADDED + KEPT, lanes] = piece
        result = jnp.dot(matrix_ref[...], pieces_in[...], preferred_element_type=jnp.float32)
        for part in range(2):
            kernel_ref[block, part] = result[:, part * LANES:(part + 1) * LANES]
        return 0

    lax.fori_loop(0, block_count, expand, 0)

    def translate_block(block):
        for parent in range(4):
            values = np.empty((2, 3, 3, 3), dtype=object)
            for part in range(2):
                for px in range(2):
                    for py in range(2):
                        for pz in range(2):
                            row = block * 256 + (2 * parent + px) * 4 + pz * 2 + py
                            values[part, px, py, pz] = spectra[part, pl.ds(row, 8, stride=32), :]
                for px in range(2):
                    for py in range(2):
                        values[part, px, py, 2] = values[part, px, py, 0] + values[part, px, py, 1]
                    for cz in range(3):
                        values[part, px, 2, cz] = values[part, px, 0, cz] + values[part, px, 1, cz]
                for cy in range(3):
                    for cz in range(3):
                        values[part, 2, cy, cz] = values[part, 0, cy, cz] + values[part, 1, cy, cz]
            for comp in range(27):
                for part in range(2):
                    value = values[part, comp // 9, comp // 3 % 3, comp % 3]
                    comps[pl.ds((parent * 10 + 1) * 54 + comp * 2 + part, 8, stride=54), :] = value

        def product(cx, cy, cz):
            comp = (cx * 3 + cy) * 3 + cz
            have = [[None, None] for _ in range(2)]
            for ey in (-1, 0, 1):
                source = []
                for parent in range(4):
                    at = (parent * 10 + 1 + ey) * 54 + comp * 2
                    source.append([comps[pl.ds(at + part, 8, stride=54), :] for part in range(2)])
                for place, (ex, neighbour_y) in enumerate(NEIGHBOURS):
                    if neighbour_y != ey:
                        continue
                    row = comp * 8 + place
                    k_re, k_im = (
                        jnp.broadcast_to(kernel_ref[block, part, row:row + 1, :], (8, LANES)) for part in range(2)
                    )
                    for parent in range(2):
                        s_re, s_im = source[parent + 1 + ex]
                        terms = (k_re * s_re - k_im * s_im, k_re * s_im + k_im * s_re)
                        for part in range(2):
                            old = have[parent][part]
                            have[parent][part] = terms[part] if old is None else old + terms[part]
            return have[0] + have[1]

        def merge(low, high, both):
            return [b + h for b, h in zip(both, high)] + [b + l for b, l in zip(both, low)]

        def along_z(cx, cy):
            return merge(product(cx, cy, 0), product(cx, cy, 1), product(cx, cy, 2))

        def along_y(cx):
            return merge(along_z(cx, 0), along_z(cx, 1), along_z(cx, 2))

        values = merge(along_y(0), along_y(1), along_y(2))
        for px in range(2):
            for py in range(2):
                for pz in range(2):
                    for parent in range(2):
                        at = ((px * 2 + py) * 2 + pz) * 4 + parent * 2
                        row = (2 * parent + px) * 4 + pz * 2 + py
                        for part in range(2):
                            sums[part, pl.ds(row, 8, stride=16), :] = values[at + part]
        for at in range(0, 128, 16):
            for part in range(2):
                split_store(split_sums, pl.multiple_of(block * 128 + at, 16), part, sums[part, at:at + 16, :])

    def one_block(block, _):
        translate_block(block)
        return 0

    lax.fori_loop(0, block_count, one_block, 0)

    for group in range(class_count):
        span = slice(group * class_blocks * 128, (group + 1) * class_blocks * 128)
        for piece in range(piece_count):
            moved[...] = jnp.dot(split_sums[span, :], tables[group * piece_count + piece, 1], preferred_element_type=jnp.float32)

            def transform_back(index, _):
                factor = factors(group * class_blocks + index, piece)
                for at in range(0, 128, 16):
                    source = pl.ds(pl.multiple_of(index * 128 + at, 16), 16)
                    full, ring = moved[source, :LANES], moved[source, LANES:]
                    full_rolled, ring_rolled = pltpu.roll(full, 64, 1), pltpu.roll(ring, 64, 1)
                    total[at:at + 16, 0:LANES] += full
                    total[at:at + 16, LANES:2 * LANES] += factor[0] * full - factor[1] * full_rolled
                    for pair in range(3):
                        lanes = slice((2 + pair) * LANES, (3 + pair) * LANES)
                        total[at:at + 16, lanes] += (
                            factor[2 + 2 * pair] * ring - factor[3 + 2 * pair] * ring_rolled
                        )
                return 0

            lax.fori_loop(0, class_blocks, transform_back, 0)

    for k, out_ref in enumerate((o0, o1, o2, o3)):
        base = pl.multiple_of((sub ^ k) * 32, 32)
        out_ref[...] = total[pl.ds(base, 32), :] * (1.0 / 4096.0)


def translate(sub_count, freq_part, chunks, inner, outer, tables, blocks):
    block_count = len(blocks)
    class_blocks = block_count * (LANES // freq_part) // tables.shape[1]
    width = COLUMNS * LANES
    matrix = jnp.asarray(np.concatenate([expansion()] * 3, axis=1), jnp.bfloat16)
    f32, bf16 = jnp.float32, jnp.bfloat16
    in_vmem = pl.BlockSpec(memory_space=pltpu.VMEM)
    anywhere = pl.BlockSpec(memory_space=pl.ANY)
    return pl.pallas_call(
        functools.partial(translate_body, sub_count, freq_part),
        in_specs=[in_vmem] * 8 + [anywhere] * (1 + block_count),
        out_specs=[in_vmem] * 4,
        scratch_shapes=[
            pltpu.VMEM((256, width), f32),
            pltpu.VMEM((256, width), f32),
            pltpu.VMEM((class_blocks * 256, 768), bf16),
            pltpu.VMEM((2, block_count * 256, LANES), f32),
            pltpu.VMEM((40 * 54, LANES), f32),
            pltpu.VMEM((2, 128, LANES), f32),
            pltpu.VMEM((block_count * 128, 768), bf16),
            pltpu.VMEM((class_blocks * 128, 256), f32),
            pltpu.VMEM((128, width), f32),
            pltpu.VMEM(tables.shape[1:], bf16),
            pltpu.VMEM((block_count, 2 * KEPT, LANES), f32),
            pltpu.VMEM((3 * KEPT_PADDED, 2 * LANES), bf16),
            pltpu.VMEM((block_count, 2, 27 * 8, LANES), f32),
            pltpu.SemaphoreType.DMA((block_count + 1,)),
        ],
        out_shape=[jax.ShapeDtypeStruct((32, width), f32)] * 4,
        compiler_params=pltpu.CompilerParams(vmem_limit_bytes=VMEM_BYTES),
        name="translate",
    )(*chunks, inner, outer, jnp.asarray(layer_factors()), matrix, tables, *blocks)


def plane_layout():
    points = surface_points(P_SIZE)
    layer = points[1:, points[0] == 1]
    at_y, at_z, used, part = (np.zeros(256, np.int32) for _ in range(4))
    at_y[:128], at_z[:128] = np.arange(128) % 64 // 8, np.arange(128) % 8
    used[:128], part[:128] = 1, np.arange(128) // 64
    for half in range(2):
        for slot in range(2):
            base = 128 + 64 * half + 32 * slot
            at_y[base:base + 28], at_z[base:base + 28] = layer
            used[base:base + 28], part[base:base + 28] = 1, half
    return at_y, at_z, used, part


def plane_tables(freq, freq_part):
    side = 2 * P_SIZE
    at_y, at_z, used, part = plane_layout()
    lib = np if isinstance(freq, np.ndarray) else jnp
    freq_y, freq_z = freq // side % side, freq % side
    column = lambda values: values[None, :, None]
    turns = column(at_y) * freq_y[:, None, :] + column(at_z) * freq_z[:, None, :]
    quarter = side // 4
    turns = lib.concatenate([turns - quarter * column(part), turns + quarter * column(1 - part)], axis=2)
    values = lib.cos((turns % side).astype(np.float32) * np.float32(2.0 * math.pi / side)) * column(used.astype(np.float32))
    pieces = LANES // freq_part
    owner = np.arange(2 * LANES) % LANES // freq_part
    mine = (owner[None, :] == np.arange(pieces)[:, None]).astype(np.float32)
    values = (values[:, None] * mine[None, :, None, :]).reshape(-1, 256, 256)
    if lib is np:
        high = values.astype(jnp.bfloat16).astype(np.float32)
    else:
        high = lax.reduce_precision(values, 8, 7)
    low = values - high
    both = []
    for turned in (False, True):
        third = [lib.swapaxes(piece, 1, 2) if turned else piece for piece in (high, high, low)]
        both.append(lib.concatenate(third, axis=1))
    return lib.stack(both, axis=1).astype(jnp.bfloat16)


def layer_factors():
    side = 2 * P_SIZE
    lane = np.arange(LANES)
    layer = np.stack([np.full(LANES, 7)] + [2 * pair + 1 + lane % 64 // 32 for pair in range(3)])
    sign = np.where(lane < 64, 1.0, -1.0)
    angles = (layer[None] * np.arange(side)[:, None, None] % side) * (2.0 * math.pi / side)
    both = np.stack([np.cos(angles), np.sin(angles) * sign], axis=2)
    return both.reshape(side, 8, LANES).astype(np.float32)


def local(density, occupied, kernels):
    block_x, block_y, block_z, surf_count = density.shape[1:]
    slab_count = lax.axis_size("slab")
    sub_count = lax.axis_size("sub")
    freq_part = kernels.shape[-1]
    assert (block_x, block_y, block_z, sub_count) == (4, 4, 2, 4)
    slab, sub = lax.axis_index("slab"), lax.axis_index("sub")
    core = slab % 2

    def exchange(values, axis, bits):
        pairs = [(i, i ^ bits) for i in range(lax.axis_size(axis))]
        return lax.ppermute(values, axis, pairs)

    own = pack(occupied, density)
    width = own.shape[-1]
    chunks = [own] + [exchange(own, "sub", k) for k in range(1, 4)]

    mine = compact_kernels(kernels)
    same_core = [mine] + [exchange(mine, "slab", m) for m in range(2, slab_count, 2)]

    same_core, chunks = lax.optimization_barrier((same_core, chunks))

    def rows_at(start):
        parts = [lax.dynamic_slice_in_dim(chunk.reshape(2, 16, width), start, 8, 1) for chunk in chunks]
        return jnp.concatenate(parts).reshape(64, width)

    across = [(i, i + 1) for i in range(1, slab_count - 1, 2)]
    across += [(right, left) for left, right in across]
    outer = lax.ppermute(rows_at(8 * core), "slab", across)
    inner = exchange(rows_at(8 * (1 - core)), "slab", 1)

    other_core = [exchange(block, "slab", 1) for block in same_core]
    pieces = LANES // freq_part
    block_count = slab_count // pieces

    def by_block(blocks):
        return [jnp.concatenate(blocks[at:at + pieces], axis=1) for at in range(0, len(blocks), pieces)]

    blocks = same_core + other_core if pieces == 1 else by_block(same_core) + by_block(other_core)
    plane = 4 * P_SIZE * P_SIZE
    if pieces == 1 and (freq_part * sub_count) % plane == 0:
        freq = np.arange(plane, dtype=np.int32).reshape(-1, LANES)
        tables = jnp.asarray(plane_tables(freq, freq_part))[:, None]
    else:
        owner = slab ^ jnp.asarray([2 * k + half for half in range(2) for k in range(pieces)], jnp.int32)
        base = freq_part * (sub_count * owner + sub)
        freq = (base[:, None] + jnp.arange(freq_part)[None, :]).reshape(2, LANES).astype(jnp.int32)
        tables = plane_tables(freq, freq_part)[None]

    parts = translate(sub_count, freq_part, chunks, inner, outer, tables, blocks)
    fields = [parts[0]] + [exchange(parts[k], "sub", k) for k in range(1, 4)]
    return unpack(occupied, fields, density.shape)


def solution(mesh):
    return jax.shard_map(
        local,
        mesh=mesh,
        in_specs=(
            P(None, "slab", "sub", None, None),
            P("slab", "sub", None),
            P(None, None, ("slab", "sub")),
        ),
        out_specs=P(None, "slab", "sub", None, None),
        check_vma=False,
    )
```

profile of v0, /device:TPU:11, one launch (start us, length us, event | category | flops | bytes accessed | tf_op | source)
XLA Modules:
  0.0 53.1 jit_solution(14239814855385230363)
XLA Ops:
  0.0 1.8 %pack.1.c0 = f32[32,640]{1,0:T(8,128)} custom-call(s32[4,2,4]{2,1,0:T(2,128)} %bitcast.17, f32[2,4,4,2,296]{4,3,2,1,0:T(2,128)} %density_ref.1), custom_call_target="tpu_custom_call" | custom-call | tf_op jit(solution)/shard_map/pack/pallas_call | solution.py:122
  1.8 1.3 %collective-permute-start.5 = (f32[32,640]{1,0:T(8,128)}, f32[32,640]{1,0:T(8,128)S(1)}, u32[]{:S(2)}, u32[]{:S(2)}) collective-permute-start(f32[32,640]{1,0:T(8,128)} %pack.1.c0), channel_id=1, source_target_pairs={{0,3},{1,2},{2,1},{3,0},{4,7},{5,6},{6,5},{7,4},{8,11},{9,10},{10,... | collective-permute-start | bytes 245768 | tf_op jit(solution)/shard_map/ppermute | solution.py:472
  3.1 1.6 %compact.1.refs_0_ = f32[240,128]{1,0:T(8,128)} custom-call(f32[632,128]{1,0:T(8,128)} %bitcast.16), custom_call_target="tpu_custom_call" | custom-call | tf_op jit(solution)/shard_map/compact/pallas_call | solution.py:76
  4.8 1.3 %collective-permute-start.2 = (f32[240,128]{1,0:T(8,128)}, f32[240,128]{1,0:T(8,128)S(1)}, u32[]{:S(2)}, u32[]{:S(2)}) collective-permute-start(f32[240,128]{1,0:T(8,128)} %compact.1.refs_0_), channel_id=1, source_target_pairs={{0,24},{4,28},{8,16},{12,20},{16,8},{20,12},{24,0},{28,4},{1,25},{... | collective-permute-start | bytes 368648 | tf_op jit(solution)/shard_map/ppermute | solution.py:472
  6.1 0.2 collective-permute-start.1
  6.3 1.2 %collective-permute-start = (f32[240,128]{1,0:T(8,128)}, f32[240,128]{1,0:T(8,128)S(1)}, u32[]{:S(2)}, u32[]{:S(2)}) collective-permute-start(f32[240,128]{1,0:T(8,128)} %compact.1.refs_0_), channel_id=1, source_target_pairs={{0,8},{4,12},{8,0},{12,4},{16,24},{20,28},{24,16},{28,20},{1,9},{5... | collective-permute-start | bytes 368648 | tf_op jit(solution)/shard_map/ppermute | solution.py:472
  7.5 1.0 %collective-permute-start.4 = (f32[32,640]{1,0:T(8,128)}, f32[32,640]{1,0:T(8,128)S(1)}, u32[]{:S(2)}, u32[]{:S(2)}) collective-permute-start(f32[32,640]{1,0:T(8,128)} %pack.1.c0), channel_id=1, source_target_pairs={{0,2},{1,3},{2,0},{3,1},{4,6},{5,7},{6,4},{7,5},{8,10},{9,11},{10,... | collective-permute-start | bytes 245768 | tf_op jit(solution)/shard_map/ppermute | solution.py:472
  8.5 1.2 %collective-permute-start.3 = (f32[32,640]{1,0:T(8,128)}, f32[32,640]{1,0:T(8,128)S(1)}, u32[]{:S(2)}, u32[]{:S(2)}) collective-permute-start(f32[32,640]{1,0:T(8,128)} %pack.1.c0), channel_id=1, source_target_pairs={{0,1},{1,0},{2,3},{3,2},{4,5},{5,4},{6,7},{7,6},{8,9},{9,8},{10,11... | collective-permute-start | bytes 245768 | tf_op jit(solution)/shard_map/ppermute | solution.py:472
  9.8 2.4 %collective-permute-done.4.c2 = f32[32,640]{1,0:T(8,128)S(1)} collective-permute-done((f32[32,640]{1,0:T(8,128)}, f32[32,640]{1,0:T(8,128)S(1)}, u32[]{:S(2)}, u32[]{:S(2)}) %collective-permute-start.4) | collective-permute-done | bytes 81952 | tf_op jit(solution)/shard_map/ppermute | solution.py:472
  12.2 0.7 %collective-permute-done.3.c1 = f32[32,640]{1,0:T(8,128)S(1)} collective-permute-done((f32[32,640]{1,0:T(8,128)}, f32[32,640]{1,0:T(8,128)S(1)}, u32[]{:S(2)}, u32[]{:S(2)}) %collective-permute-start.3) | collective-permute-done | bytes 81952 | tf_op jit(solution)/shard_map/ppermute | solution.py:472
  12.9 0.0 collective-permute-done.2.refs_3_
  12.9 0.6 %collective-permute-done.1.refs_2_ = f32[240,128]{1,0:T(8,128)S(1)} collective-permute-done((f32[240,128]{1,0:T(8,128)}, f32[240,128]{1,0:T(8,128)S(1)}, u32[]{:S(2)}, u32[]{:S(2)}) %collective-permute-start.1) | collective-permute-done | bytes 122912 | tf_op jit(solution)/shard_map/ppermute | solution.py:472
  13.5 2.4 %collective-permute-start.8 = (f32[240,128]{1,0:T(8,128)}, f32[240,128]{1,0:T(8,128)S(1)}, u32[]{:S(2)}, u32[]{:S(2)}) collective-permute-start(f32[240,128]{1,0:T(8,128)} %compact.1.refs_0_), channel_id=1, source_target_pairs={{0,4},{4,0},{8,12},{12,8},{16,20},{20,16},{24,28},{28,24},{1,5},{5... | collective-permute-start | bytes 368648 | tf_op jit(solution)/shard_map/ppermute | solution.py:472
  15.9 0.8 %constant_dynamic-slice_fusion.2 = (f32[2,8,640]{2,1,0:T(8,128)S(1)}, f32[2,8,640]{2,1,0:T(8,128)S(1)}, f32[2,8,640]{2,1,0:T(8,128)S(1)}, f32[2,8,640]{2,1,0:T(8,128)S(1)}) fusion(f32[2,16,640]{2,1,0:T(8,128)S(1)} %bitcast.15, s32[]{:T(128)S(6)} %select_n.21, s32[]{:T(128)S(6)} %select_n.20, f32[2,16,640]{2,1,0:T(8,128)} %bitcast.12), kind=kLoop, calls=%fused_computation.4 | loop fusion | bytes 327688 | tf_op jit(solution)/shard_map/dynamic_slice | solution.py:484
  16.8 0.1 collective-permute-start.6
  16.9 3.5 %collective-permute-start.7 = (f32[64,640]{1,0:T(8,128)S(1)}, f32[64,640]{1,0:T(8,128)S(1)}, u32[]{:S(2)}, u32[]{:S(2)}) collective-permute-start(f32[64,640]{1,0:T(8,128)S(1)} %maximum_bitcast_fusion.1), channel_id=1, source_target_pairs={{4,8},{12,16},{20,24},{8,4},{16,12},{24,20},{5,9},{13,17},{21,25},... | collective-permute-start | bytes 491528 | tf_op jit(solution)/shard_map/ppermute | solution.py:489
  20.4 0.1 collective-permute-start.9
  20.4 0.5 collective-permute-start.10
  20.9 0.1 collective-permute-start.11
  21.0 0.7 %collective-permute-done.9.refs_5_ = f32[240,128]{1,0:T(8,128)S(1)} collective-permute-done((f32[240,128]{1,0:T(8,128)S(1)}, f32[240,128]{1,0:T(8,128)S(1)}, u32[]{:S(2)}, u32[]{:S(2)}) %collective-permute-start.9) | collective-permute-done | bytes 122912 | tf_op jit(solution)/shard_map/ppermute | solution.py:472
  21.8 0.2 collective-permute-done.10.refs_6_
  21.9 0.3 collective-permute-done.11.refs_7_
  22.3 3.7 %collective-permute-done.7.outer_ref = f32[64,640]{1,0:T(8,128)S(1)} collective-permute-done((f32[64,640]{1,0:T(8,128)S(1)}, f32[64,640]{1,0:T(8,128)S(1)}, u32[]{:S(2)}, u32[]{:S(2)}) %collective-permute-start.7) | collective-permute-done | bytes 163872 | tf_op jit(solution)/shard_map/ppermute | solution.py:489
  26.1 0.6 %copy-done.4 = f32[64,640]{1,0:T(8,128)} copy-done((f32[64,640]{1,0:T(8,128)}, f32[64,640]{1,0:T(8,128)S(1)}, u32[]{:S(2)}) %copy-start.4) | copy-done | bytes 163864
  26.8 13.8 %translate.1 = (f32[32,640]{1,0:T(8,128)}, f32[32,640]{1,0:T(8,128)}, f32[32,640]{1,0:T(8,128)}, f32[32,640]{1,0:T(8,128)}) custom-call(f32[32,640]{1,0:T(8,128)} %pack.1.c0, f32[32,640]{1,0:T(8,128)} %copy-done.2, f32[32,640]{1,0:T(8,128)} %copy-done.1, f32[32,640]{1,0:T(8,128)} %copy-done, f32[64,640]{1,0:T(8,128)} %copy-done.3, f32[64,640]{1,0:T(8,128)} %copy-done.4, ...), custom_call_target="tpu_custom_call" | custom-call | tf_op jit(solution)/shard_map/translate/pallas_call | solution.py:385
  40.6 1.7 %collective-permute-start.12 = (f32[32,640]{1,0:T(8,128)}, f32[32,640]{1,0:T(8,128)S(1)}, u32[]{:S(2)}, u32[]{:S(2)}) collective-permute-start(f32[32,640]{1,0:T(8,128)} %get-tuple-element.26), channel_id=1, source_target_pairs={{0,1},{1,0},{2,3},{3,2},{4,5},{5,4},{6,7},{7,6},{8,9},{9,8},{10,11... | collective-permute-start | bytes 245768 | tf_op jit(solution)/shard_map/ppermute | solution.py:472
  42.3 1.4 %collective-permute-start.13 = (f32[32,640]{1,0:T(8,128)}, f32[32,640]{1,0:T(8,128)S(1)}, u32[]{:S(2)}, u32[]{:S(2)}) collective-permute-start(f32[32,640]{1,0:T(8,128)} %get-tuple-element.27), channel_id=1, source_target_pairs={{0,2},{1,3},{2,0},{3,1},{4,6},{5,7},{6,4},{7,5},{8,10},{9,11},{10,... | collective-permute-start | bytes 245768 | tf_op jit(solution)/shard_map/ppermute | solution.py:472
  43.6 1.8 %collective-permute-done.12.p1 = f32[32,640]{1,0:T(8,128)S(1)} collective-permute-done((f32[32,640]{1,0:T(8,128)}, f32[32,640]{1,0:T(8,128)S(1)}, u32[]{:S(2)}, u32[]{:S(2)}) %collective-permute-start.12) | collective-permute-done | bytes 81952 | tf_op jit(solution)/shard_map/ppermute | solution.py:472
  45.4 3.5 %collective-permute-done.13.p2 = f32[32,640]{1,0:T(8,128)S(1)} collective-permute-done((f32[32,640]{1,0:T(8,128)}, f32[32,640]{1,0:T(8,128)S(1)}, u32[]{:S(2)}, u32[]{:S(2)}) %collective-permute-start.13) | collective-permute-done | bytes 81952 | tf_op jit(solution)/shard_map/ppermute | solution.py:472
  48.9 1.8 %collective-permute-done.14.p3 = f32[32,640]{1,0:T(8,128)S(1)} collective-permute-done((f32[32,640]{1,0:T(8,128)}, f32[32,640]{1,0:T(8,128)S(1)}, u32[]{:S(2)}, u32[]{:S(2)}) %collective-permute-start.14) | collective-permute-done | bytes 81952 | tf_op jit(solution)/shard_map/ppermute | solution.py:472
  50.7 0.6 %copy-done.14 = f32[32,640]{1,0:T(8,128)} copy-done((f32[32,640]{1,0:T(8,128)}, f32[32,640]{1,0:T(8,128)S(1)}, u32[]{:S(2)}) %copy-start.14) | copy-done | bytes 81944
  51.3 1.9 %unpack.1 = f32[2,4,4,2,296]{4,3,2,1,0:T(2,128)} custom-call(s32[4,2,4]{2,1,0:T(2,128)} %bitcast.18, f32[32,640]{1,0:T(8,128)} %get-tuple-element.25.p0, f32[32,640]{1,0:T(8,128)} %copy-done.12, f32[32,640]{1,0:T(8,128)} %copy-done.13, f32[32,640]{1,0:T(8,128)} %copy-done.14), custom_call_target="tpu_custom_call" | custom-call | tf_op jit(solution)/shard_map/unpack/pallas_call | solution.py:153
  (36 shorter events, 0.1 us)
Async XLA Ops:
  1.8 6.7 %collective-permute-start.5 = (f32[32,640]{1,0:T(8,128)}, f32[32,640]{1,0:T(8,128)S(1)}, u32[]{:S(2)}, u32[]{:S(2)}) collective-permute-start(f32[32,640]{1,0:T(8,128)} %pack.1.c0), channel_id=1, source_target_pairs={{0,3},{1,2},{2,1},{3,0},{4,7},{5,6},{6,5},{7,4},{8,11},{9,10},{10,... | collective-permute-start | bytes 245768 | tf_op jit(solution)/shard_map/ppermute | solution.py:472
  4.8 8.1 %collective-permute-start.2 = (f32[240,128]{1,0:T(8,128)}, f32[240,128]{1,0:T(8,128)S(1)}, u32[]{:S(2)}, u32[]{:S(2)}) collective-permute-start(f32[240,128]{1,0:T(8,128)} %compact.1.refs_0_), channel_id=1, source_target_pairs={{0,24},{4,28},{8,16},{12,20},{16,8},{20,12},{24,0},{28,4},{1,25},{... | collective-permute-start | bytes 368648 | tf_op jit(solution)/shard_map/ppermute | solution.py:472
  6.1 7.5 %collective-permute-start.1 = (f32[240,128]{1,0:T(8,128)}, f32[240,128]{1,0:T(8,128)S(1)}, u32[]{:S(2)}, u32[]{:S(2)}) collective-permute-start(f32[240,128]{1,0:T(8,128)} %compact.1.refs_0_), channel_id=1, source_target_pairs={{0,16},{4,20},{8,24},{12,28},{16,0},{20,4},{24,8},{28,12},{1,17},{... | collective-permute-start | bytes 368648 | tf_op jit(solution)/shard_map/ppermute | solution.py:472
  6.3 7.2 %collective-permute-start = (f32[240,128]{1,0:T(8,128)}, f32[240,128]{1,0:T(8,128)S(1)}, u32[]{:S(2)}, u32[]{:S(2)}) collective-permute-start(f32[240,128]{1,0:T(8,128)} %compact.1.refs_0_), channel_id=1, source_target_pairs={{0,8},{4,12},{8,0},{12,4},{16,24},{20,28},{24,16},{28,20},{1,9},{5... | collective-permute-start | bytes 368648 | tf_op jit(solution)/shard_map/ppermute | solution.py:472
  7.5 4.7 %collective-permute-start.4 = (f32[32,640]{1,0:T(8,128)}, f32[32,640]{1,0:T(8,128)S(1)}, u32[]{:S(2)}, u32[]{:S(2)}) collective-permute-start(f32[32,640]{1,0:T(8,128)} %pack.1.c0), channel_id=1, source_target_pairs={{0,2},{1,3},{2,0},{3,1},{4,6},{5,7},{6,4},{7,5},{8,10},{9,11},{10,... | collective-permute-start | bytes 245768 | tf_op jit(solution)/shard_map/ppermute | solution.py:472
  8.5 17.5 %copy-start = (f32[32,640]{1,0:T(8,128)}, f32[32,640]{1,0:T(8,128)S(1)}, u32[]{:S(2)}) copy-start(f32[32,640]{1,0:T(8,128)S(1)} %collective-permute-done.5.c3) | copy-start | bytes 245764
  8.5 4.4 %collective-permute-start.3 = (f32[32,640]{1,0:T(8,128)}, f32[32,640]{1,0:T(8,128)S(1)}, u32[]{:S(2)}, u32[]{:S(2)}) collective-permute-start(f32[32,640]{1,0:T(8,128)} %pack.1.c0), channel_id=1, source_target_pairs={{0,1},{1,0},{2,3},{3,2},{4,5},{5,4},{6,7},{7,6},{8,9},{9,8},{10,11... | collective-permute-start | bytes 245768 | tf_op jit(solution)/shard_map/ppermute | solution.py:472
  12.2 13.8 %copy-start.1 = (f32[32,640]{1,0:T(8,128)}, f32[32,640]{1,0:T(8,128)S(1)}, u32[]{:S(2)}) copy-start(f32[32,640]{1,0:T(8,128)S(1)} %collective-permute-done.4.c2) | copy-start | bytes 245764
  12.9 13.1 %copy-start.2 = (f32[32,640]{1,0:T(8,128)}, f32[32,640]{1,0:T(8,128)S(1)}, u32[]{:S(2)}) copy-start(f32[32,640]{1,0:T(8,128)S(1)} %collective-permute-done.3.c1) | copy-start | bytes 245764
  12.9 13.1 %copy-start.5 = (f32[240,128]{1,0:T(8,128)}, f32[240,128]{1,0:T(8,128)S(1)}, u32[]{:S(2)}) copy-start(f32[240,128]{1,0:T(8,128)S(1)} %collective-permute-done.2.refs_3_) | copy-start | bytes 368644
  13.5 12.5 %copy-start.6 = (f32[240,128]{1,0:T(8,128)}, f32[240,128]{1,0:T(8,128)S(1)}, u32[]{:S(2)}) copy-start(f32[240,128]{1,0:T(8,128)S(1)} %collective-permute-done.1.refs_2_) | copy-start | bytes 368644
  13.5 12.5 %copy-start.7 = (f32[240,128]{1,0:T(8,128)}, f32[240,128]{1,0:T(8,128)S(1)}, u32[]{:S(2)}) copy-start(f32[240,128]{1,0:T(8,128)S(1)} %collective-permute-done.refs_1_) | copy-start | bytes 368644
  13.5 7.4 %collective-permute-start.8 = (f32[240,128]{1,0:T(8,128)}, f32[240,128]{1,0:T(8,128)S(1)}, u32[]{:S(2)}, u32[]{:S(2)}) collective-permute-start(f32[240,128]{1,0:T(8,128)} %compact.1.refs_0_), channel_id=1, source_target_pairs={{0,4},{4,0},{8,12},{12,8},{16,20},{20,16},{24,28},{28,24},{1,5},{5... | collective-permute-start | bytes 368648 | tf_op jit(solution)/shard_map/ppermute | solution.py:472
  16.8 5.5 %collective-permute-start.6 = (f32[64,640]{1,0:T(8,128)S(1)}, f32[64,640]{1,0:T(8,128)S(1)}, u32[]{:S(2)}, u32[]{:S(2)}) collective-permute-start(f32[64,640]{1,0:T(8,128)S(1)} %maximum_bitcast_fusion), channel_id=1, source_target_pairs={{0,4},{4,0},{8,12},{12,8},{16,20},{20,16},{24,28},{28,24},{1,5},{5... | collective-permute-start | bytes 491528 | tf_op jit(solution)/shard_map/ppermute | solution.py:472
  16.9 9.1 %collective-permute-start.7 = (f32[64,640]{1,0:T(8,128)S(1)}, f32[64,640]{1,0:T(8,128)S(1)}, u32[]{:S(2)}, u32[]{:S(2)}) collective-permute-start(f32[64,640]{1,0:T(8,128)S(1)} %maximum_bitcast_fusion.1), channel_id=1, source_target_pairs={{4,8},{12,16},{20,24},{8,4},{16,12},{24,20},{5,9},{13,17},{21,25},... | collective-permute-start | bytes 491528 | tf_op jit(solution)/shard_map/ppermute | solution.py:489
  20.4 1.4 %collective-permute-start.9 = (f32[240,128]{1,0:T(8,128)S(1)}, f32[240,128]{1,0:T(8,128)S(1)}, u32[]{:S(2)}, u32[]{:S(2)}) collective-permute-start(f32[240,128]{1,0:T(8,128)S(1)} %collective-permute-done.refs_1_), channel_id=1, source_target_pairs={{0,4},{4,0},{8,12},{12,8},{16,20},{20,16},{24,28},{28,24},{1,5},{5... | collective-permute-start | bytes 368648 | tf_op jit(solution)/shard_map/ppermute | solution.py:472
  20.4 1.5 %collective-permute-start.10 = (f32[240,128]{1,0:T(8,128)S(1)}, f32[240,128]{1,0:T(8,128)S(1)}, u32[]{:S(2)}, u32[]{:S(2)}) collective-permute-start(f32[240,128]{1,0:T(8,128)S(1)} %collective-permute-done.1.refs_2_), channel_id=1, source_target_pairs={{0,4},{4,0},{8,12},{12,8},{16,20},{20,16},{24,28},{28,24},{1,5},{5... | collective-permute-start | bytes 368648 | tf_op jit(solution)/shard_map/ppermute | solution.py:472
  20.9 5.1 %copy-start.8 = (f32[240,128]{1,0:T(8,128)}, f32[240,128]{1,0:T(8,128)S(1)}, u32[]{:S(2)}) copy-start(f32[240,128]{1,0:T(8,128)S(1)} %collective-permute-done.8.refs_4_) | copy-start | bytes 368644
  20.9 1.3 %collective-permute-start.11 = (f32[240,128]{1,0:T(8,128)S(1)}, f32[240,128]{1,0:T(8,128)S(1)}, u32[]{:S(2)}, u32[]{:S(2)}) collective-permute-start(f32[240,128]{1,0:T(8,128)S(1)} %collective-permute-done.2.refs_3_), channel_id=1, source_target_pairs={{0,4},{4,0},{8,12},{12,8},{16,20},{20,16},{24,28},{28,24},{1,5},{5... | collective-permute-start | bytes 368648 | tf_op jit(solution)/shard_map/ppermute | solution.py:472
  21.8 4.3 %copy-start.9 = (f32[240,128]{1,0:T(8,128)}, f32[240,128]{1,0:T(8,128)S(1)}, u32[]{:S(2)}) copy-start(f32[240,128]{1,0:T(8,128)S(1)} %collective-permute-done.9.refs_5_) | copy-start | bytes 368644
  21.9 4.1 %copy-start.10 = (f32[240,128]{1,0:T(8,128)}, f32[240,128]{1,0:T(8,128)S(1)}, u32[]{:S(2)}) copy-start(f32[240,128]{1,0:T(8,128)S(1)} %collective-permute-done.10.refs_6_) | copy-start | bytes 368644
  22.3 3.8 %copy-start.11 = (f32[240,128]{1,0:T(8,128)}, f32[240,128]{1,0:T(8,128)S(1)}, u32[]{:S(2)}) copy-start(f32[240,128]{1,0:T(8,128)S(1)} %collective-permute-done.11.refs_7_) | copy-start | bytes 368644
  22.3 3.8 %copy-start.3 = (f32[64,640]{1,0:T(8,128)}, f32[64,640]{1,0:T(8,128)S(1)}, u32[]{:S(2)}) copy-start(f32[64,640]{1,0:T(8,128)S(1)} %collective-permute-done.6.inner_ref) | copy-start | bytes 491524
  26.1 0.7 %copy-start.4 = (f32[64,640]{1,0:T(8,128)}, f32[64,640]{1,0:T(8,128)S(1)}, u32[]{:S(2)}) copy-start(f32[64,640]{1,0:T(8,128)S(1)} %collective-permute-done.7.outer_ref) | copy-start | bytes 491524
  40.6 4.8 %collective-permute-start.12 = (f32[32,640]{1,0:T(8,128)}, f32[32,640]{1,0:T(8,128)S(1)}, u32[]{:S(2)}, u32[]{:S(2)}) collective-permute-start(f32[32,640]{1,0:T(8,128)} %get-tuple-element.26), channel_id=1, source_target_pairs={{0,1},{1,0},{2,3},{3,2},{4,5},{5,4},{6,7},{7,6},{8,9},{9,8},{10,11... | collective-permute-start | bytes 245768 | tf_op jit(solution)/shard_map/ppermute | solution.py:472
  42.3 6.6 %collective-permute-start.13 = (f32[32,640]{1,0:T(8,128)}, f32[32,640]{1,0:T(8,128)S(1)}, u32[]{:S(2)}, u32[]{:S(2)}) collective-permute-start(f32[32,640]{1,0:T(8,128)} %get-tuple-element.27), channel_id=1, source_target_pairs={{0,2},{1,3},{2,0},{3,1},{4,6},{5,7},{6,4},{7,5},{8,10},{9,11},{10,... | collective-permute-start | bytes 245768 | tf_op jit(solution)/shard_map/ppermute | solution.py:472
  43.6 7.0 %collective-permute-start.14 = (f32[32,640]{1,0:T(8,128)}, f32[32,640]{1,0:T(8,128)S(1)}, u32[]{:S(2)}, u32[]{:S(2)}) collective-permute-start(f32[32,640]{1,0:T(8,128)} %get-tuple-element.28), channel_id=1, source_target_pairs={{0,3},{1,2},{2,1},{3,0},{4,7},{5,6},{6,5},{7,4},{8,11},{9,10},{10,... | collective-permute-start | bytes 245768 | tf_op jit(solution)/shard_map/ppermute | solution.py:472
  45.4 5.2 %copy-start.12 = (f32[32,640]{1,0:T(8,128)}, f32[32,640]{1,0:T(8,128)S(1)}, u32[]{:S(2)}) copy-start(f32[32,640]{1,0:T(8,128)S(1)} %collective-permute-done.12.p1) | copy-start | bytes 245764
  48.9 1.8 %copy-start.13 = (f32[32,640]{1,0:T(8,128)}, f32[32,640]{1,0:T(8,128)S(1)}, u32[]{:S(2)}) copy-start(f32[32,640]{1,0:T(8,128)S(1)} %collective-permute-done.13.p2) | copy-start | bytes 245764
  50.6 0.6 %copy-start.14 = (f32[32,640]{1,0:T(8,128)}, f32[32,640]{1,0:T(8,128)S(1)}, u32[]{:S(2)}) copy-start(f32[32,640]{1,0:T(8,128)S(1)} %collective-permute-done.14.p3) | copy-start | bytes 245764
where the time goes:
time: 53.5 us; the launch traced here: 53.1 us
  Pallas kernels  19.1 us (36%)
  starting transfers between devices  16 us (30%)
  waiting for transfers between devices  15.7 us (29%)
  local copies, waits for them, and re-layouts  2.15 us (4%)
    pallas_call x1, Pallas kernels, translate(): pl.pallas_call(functools.partial(translate_body, sub_count, freq_part), i...  13.8 us
    ppermute x14, starting transfers between devices, exchange(): return lax.ppermute(values, axis, pairs)  12.5 us
    ppermute x14, waiting for transfers between devices, exchange(): return lax.ppermute(values, axis, pairs)  12 us
    ppermute x1, waiting for transfers between devices, local(): outer = lax.ppermute(rows_at(8 * core), 'slab', across)  3.72 us
    ppermute x1, starting transfers between devices, local(): outer = lax.ppermute(rows_at(8 * core), 'slab', across)  3.47 us
    pallas_call x1, Pallas kernels, unpack(): pl.pallas_call(unpack_body, in_specs=[pl.BlockSpec(memory_space=pltpu.VME...  1.87 us
    pallas_call x1, Pallas kernels, pack(): pl.pallas_call(pack_body, in_specs=[pl.BlockSpec(memory_space=pltpu.VMEM)...  1.84 us
    pallas_call x1, Pallas kernels, compact_kernels(): pl.pallas_call(compact_body, in_specs=[pl.BlockSpec(memory_space=pl.ANY)]...  1.64 us
  transfers between devices with their start and end apart: 15, of which 10 were waited for; matrix products, arithmetic and copies ran while one was open for 2% of the time, Pallas kernels for 3%

commit v1 on v0

--- a/solution.py
+++ b/solution.py
@@ -170,10 +170,10 @@
     sub_count, freq_part,
     c0, c1, c2, c3, inner_ref, outer_ref, factor_ref, matrix_ref, table_ref, *refs,
 ):
-    block_count = len(refs) - 4 - 14
+    block_count = len(refs) - 4 - 13
     block_refs, (o0, o1, o2, o3) = refs[:block_count], refs[block_count:block_count + 4]
     (
-        rows, rolled, layers, spectra, comps, sums, split_sums, moved, total, tables, raw, pieces_in, kernel_ref, sems,
+        rows, rolled, layers, spectra, comps, sums, split_sums, moved, total, tables, pieces_in, kernel_ref, sem,
     ) = refs[block_count + 4:]
     slab, sub = lax.axis_index("slab"), lax.axis_index("sub")
     core = lax.rem(slab, 2)
@@ -184,11 +184,8 @@
     plane = 4 * P_SIZE * P_SIZE
 
     variant = lax.div(lax.rem(freq_part * sub, plane), LANES) if table_ref.shape[0] > 1 else 0
-    copies = [pltpu.make_async_copy(table_ref.at[variant], tables, sems.at[block_count])]
-    for block, ref in enumerate(block_refs):
-        copies.append(pltpu.make_async_copy(ref, raw.at[block], sems.at[block]))
-    for copy in copies:
-        copy.start()
+    copy = pltpu.make_async_copy(table_ref.at[variant], tables, sem)
+    copy.start()
 
     for k, chunk in enumerate((c0, c1, c2, c3)):
         source = sub ^ k
@@ -247,7 +244,7 @@
 
             lax.fori_loop(0, class_blocks, transform_x, 0)
             if group == 0 and piece == 0:
-                copies[0].wait()
+                copy.wait()
             found = jnp.dot(layers[...], tables[group * piece_count + piece, 0], preferred_element_type=jnp.float32)
             span = slice(group * class_blocks * 256, (group + 1) * class_blocks * 256)
             for part in range(2):
@@ -256,23 +253,17 @@
                     values = values + spectra[part, span, :]
                 spectra[part, span, :] = values
 
-    for copy in copies[1:]:
-        copy.wait()
-
-    def expand(block, _):
+    for block in range(block_count):
         for part in range(2):
-            left = raw[block, pl.ds(part, KEPT, stride=2), :]
+            left = block_refs[block][pl.ds(part, KEPT, stride=2), :]
             lanes = slice(part * LANES, (part + 1) * LANES)
             for turn in range(3):
                 piece = left.astype(jnp.bfloat16)
                 left = left - piece.astype(jnp.float32)
-                pieces_in[turn * KEPT_PADDED:turn * KEPT_PADDED + KEPT, lanes] = piece
-        result = jnp.dot(matrix_ref[...], pieces_in[...], preferred_element_type=jnp.float32)
+                pieces_in[block % 2, turn * KEPT_PADDED:turn * KEPT_PADDED + KEPT, lanes] = piece
+        result = jnp.dot(matrix_ref[...], pieces_in[block % 2], preferred_element_type=jnp.float32)
         for part in range(2):
             kernel_ref[block, part] = result[:, part * LANES:(part + 1) * LANES]
-        return 0
-
-    lax.fori_loop(0, block_count, expand, 0)
 
     def translate_block(block):
         for parent in range(4):
@@ -384,7 +375,7 @@
     anywhere = pl.BlockSpec(memory_space=pl.ANY)
     return pl.pallas_call(
         functools.partial(translate_body, sub_count, freq_part),
-        in_specs=[in_vmem] * 8 + [anywhere] * (1 + block_count),
+        in_specs=[in_vmem] * 8 + [anywhere] + [in_vmem] * block_count,
         out_specs=[in_vmem] * 4,
         scratch_shapes=[
             pltpu.VMEM((256, width), f32),
@@ -397,10 +388,9 @@
             pltpu.VMEM((class_blocks * 128, 256), f32),
             pltpu.VMEM((128, width), f32),
             pltpu.VMEM(tables.shape[1:], bf16),
-            pltpu.VMEM((block_count, 2 * KEPT, LANES), f32),
-            pltpu.VMEM((3 * KEPT_PADDED, 2 * LANES), bf16),
+            pltpu.VMEM((2, 3 * KEPT_PADDED, 2 * LANES), bf16),
             pltpu.VMEM((block_count, 2, 27 * 8, LANES), f32),
-            pltpu.SemaphoreType.DMA((block_count + 1,)),
+            pltpu.SemaphoreType.DMA,
         ],
         out_shape=[jax.ShapeDtypeStruct((32, width), f32)] * 4,
         compiler_params=pltpu.CompilerParams(vmem_limit_bytes=VMEM_BYTES),
@@ -471,14 +461,11 @@
         pairs = [(i, i ^ bits) for i in range(lax.axis_size(axis))]
         return lax.ppermute(values, axis, pairs)
 
-    own = pack(occupied, density)
+    own, mine = pack(occupied, density), compact_kernels(kernels)
     width = own.shape[-1]
     chunks = [own] + [exchange(own, "sub", k) for k in range(1, 4)]
 
-    mine = compact_kernels(kernels)
     same_core = [mine] + [exchange(mine, "slab", m) for m in range(2, slab_count, 2)]
-
-    same_core, chunks = lax.optimization_barrier((same_core, chunks))
 
     def rows_at(start):
         parts = [lax.dynamic_slice_in_dim(chunk.reshape(2, 16, width), start, 8, 1) for chunk in chunks]
@@ -486,8 +473,10 @@
 
     across = [(i, i + 1) for i in range(1, slab_count - 1, 2)]
     across += [(right, left) for left, right in across]
-    outer = lax.ppermute(rows_at(8 * core), "slab", across)
-    inner = exchange(rows_at(8 * (1 - core)), "slab", 1)
+    outer, inner = rows_at(8 * core), rows_at(8 * (1 - core))
+    outer, inner, same_core = lax.optimization_barrier((outer, inner, same_core))
+    outer = lax.ppermute(outer, "slab", across)
+    inner = exchange(inner, "slab", 1)
 
     other_core = [exchange(block, "slab", 1) for block in same_core]
     pieces = LANES // freq_part
@@ -508,7 +497,7 @@
         tables = plane_tables(freq, freq_part)[None]
 
     parts = translate(sub_count, freq_part, chunks, inner, outer, tables, blocks)
-    fields = [parts[0]] + [exchange(parts[k], "sub", k) for k in range(1, 4)]
+    fields = [parts[0]] + [exchange(parts[k], "sub", k) for k in (3, 2, 1)]
     return unpack(occupied, fields, density.shape)
 
 

time: 53.5 us -> 52.5 us (0.981)
  the two profiles are of different devices: /device:TPU:11 before, /device:TPU:0 now
where the time goes in v1:
time: 52.5 us; the launch traced here: 52.1 us
  Pallas kernels  18.7 us (36%)
  starting transfers between devices  17.5 us (33%)
  waiting for transfers between devices  12.9 us (25%)
  local copies, waits for them, and re-layouts  2.79 us (5%)
    ppermute x14, starting transfers between devices, exchange(): return lax.ppermute(values, axis, pairs)  16.8 us
    pallas_call x1, Pallas kernels, translate(): pl.pallas_call(functools.partial(translate_body, sub_count, freq_part), i...  13.4 us
    ppermute x14, waiting for transfers between devices, exchange(): return lax.ppermute(values, axis, pairs)  12.9 us
    unnamed x30, local copies, waits for them, and re-layouts  1.95 us
    pallas_call x1, Pallas kernels, unpack(): pl.pallas_call(unpack_body, in_specs=[pl.BlockSpec(memory_space=pltpu.VME...  1.87 us
    pallas_call x1, Pallas kernels, pack(): pl.pallas_call(pack_body, in_specs=[pl.BlockSpec(memory_space=pltpu.VMEM)...  1.84 us
    pallas_call x1, Pallas kernels, compact_kernels(): pl.pallas_call(compact_body, in_specs=[pl.BlockSpec(memory_space=pl.ANY)]...  1.65 us
  transfers between devices with their start and end apart: 15, of which 9 were waited for; matrix products, arithmetic and copies ran while one was open for 2% of the time, Pallas kernels for 3%

profile of v1, /device:TPU:0, one launch (start us, length us, event | category | flops | bytes accessed | tf_op | source)
XLA Modules:
  0.0 52.1 jit_solution(15785093691114036578)
XLA Ops:
  0.0 1.8 %pack.1.c0 = f32[32,640]{1,0:T(8,128)} custom-call(s32[4,2,4]{2,1,0:T(2,128)} %bitcast.17, f32[2,4,4,2,296]{4,3,2,1,0:T(2,128)} %density_ref.1), custom_call_target="tpu_custom_call" | custom-call | tf_op jit(solution)/shard_map/pack/pallas_call | solution.py:122
  1.8 5.0 %collective-permute-start.2 = (f32[32,640]{1,0:T(8,128)}, f32[32,640]{1,0:T(8,128)S(1)}, u32[]{:S(2)}, u32[]{:S(2)}) collective-permute-start(f32[32,640]{1,0:T(8,128)} %pack.1.c0), channel_id=1, source_target_pairs={{0,3},{1,2},{2,1},{3,0},{4,7},{5,6},{6,5},{7,4},{8,11},{9,10},{10,... | collective-permute-start | bytes 245768 | tf_op jit(solution)/shard_map/ppermute | solution.py:462
  6.9 0.6 %collective-permute-start = (f32[32,640]{1,0:T(8,128)}, f32[32,640]{1,0:T(8,128)S(1)}, u32[]{:S(2)}, u32[]{:S(2)}) collective-permute-start(f32[32,640]{1,0:T(8,128)} %pack.1.c0), channel_id=1, source_target_pairs={{0,1},{1,0},{2,3},{3,2},{4,5},{5,4},{6,7},{7,6},{8,9},{9,8},{10,11... | collective-permute-start | bytes 245768 | tf_op jit(solution)/shard_map/ppermute | solution.py:462
  7.5 1.7 %compact.1.refs_0_ = f32[240,128]{1,0:T(8,128)} custom-call(f32[632,128]{1,0:T(8,128)} %bitcast.16), custom_call_target="tpu_custom_call" | custom-call | tf_op jit(solution)/shard_map/compact/pallas_call | solution.py:76
  9.1 2.7 %collective-permute-start.5 = (f32[240,128]{1,0:T(8,128)}, f32[240,128]{1,0:T(8,128)S(1)}, u32[]{:S(2)}, u32[]{:S(2)}) collective-permute-start(f32[240,128]{1,0:T(8,128)} %compact.1.refs_0_), channel_id=1, source_target_pairs={{0,24},{4,28},{8,16},{12,20},{16,8},{20,12},{24,0},{28,4},{1,25},{... | collective-permute-start | bytes 368648 | tf_op jit(solution)/shard_map/ppermute | solution.py:462
  11.9 0.5 collective-permute-start.4
  12.4 0.8 %constant_dynamic-slice_fusion.3 = (f32[2,8,640]{2,1,0:T(8,128)S(1)}, f32[2,8,640]{2,1,0:T(8,128)S(1)}) fusion(f32[2,16,640]{2,1,0:T(8,128)} %bitcast.12, s32[]{:T(128)S(6)} %select_n.21, s32[]{:T(128)S(6)} %select_n.20), kind=kLoop, calls=%fused_computation.5 | loop fusion | bytes 163848 | tf_op jit(solution)/shard_map/dynamic_slice | solution.py:471
  13.2 0.4 collective-permute-start.3
  13.6 0.4 collective-permute-done.1.c2
  14.1 1.3 %collective-permute-done.5.refs_3_ = f32[240,128]{1,0:T(8,128)S(1)} collective-permute-done((f32[240,128]{1,0:T(8,128)}, f32[240,128]{1,0:T(8,128)S(1)}, u32[]{:S(2)}, u32[]{:S(2)}) %collective-permute-start.5) | collective-permute-done | bytes 122912 | tf_op jit(solution)/shard_map/ppermute | solution.py:462
  15.3 2.1 %collective-permute-done.4.refs_2_ = f32[240,128]{1,0:T(8,128)S(1)} collective-permute-done((f32[240,128]{1,0:T(8,128)}, f32[240,128]{1,0:T(8,128)S(1)}, u32[]{:S(2)}, u32[]{:S(2)}) %collective-permute-start.4) | collective-permute-done | bytes 122912 | tf_op jit(solution)/shard_map/ppermute | solution.py:462
  17.4 0.9 %collective-permute-done.3.refs_1_ = f32[240,128]{1,0:T(8,128)S(1)} collective-permute-done((f32[240,128]{1,0:T(8,128)}, f32[240,128]{1,0:T(8,128)S(1)}, u32[]{:S(2)}, u32[]{:S(2)}) %collective-permute-start.3) | collective-permute-done | bytes 122912 | tf_op jit(solution)/shard_map/ppermute | solution.py:462
  18.3 0.5 collective-permute-start.6
  18.8 0.7 %collective-permute-start.7 = (f32[64,640]{1,0:T(8,128)S(1)}, f32[64,640]{1,0:T(8,128)S(1)}, u32[]{:S(2)}, u32[]{:S(2)}) collective-permute-start(f32[64,640]{1,0:T(8,128)S(1)} %get-tuple-element.16), channel_id=1, source_target_pairs={{4,8},{12,16},{20,24},{8,4},{16,12},{24,20},{5,9},{13,17},{21,25},... | collective-permute-start | bytes 491528 | tf_op jit(solution)/shard_map/ppermute | solution.py:478
  19.5 2.1 %collective-permute-start.9 = (f32[240,128]{1,0:T(8,128)S(1)}, f32[240,128]{1,0:T(8,128)S(1)}, u32[]{:S(2)}, u32[]{:S(2)}) collective-permute-start(f32[240,128]{1,0:T(8,128)S(1)} %collective-permute-done.3.refs_1_), channel_id=1, source_target_pairs={{0,4},{4,0},{8,12},{12,8},{16,20},{20,16},{24,28},{28,24},{1,5},{5... | collective-permute-start | bytes 368648 | tf_op jit(solution)/shard_map/ppermute | solution.py:462
  21.6 0.1 collective-permute-start.10
  21.7 0.4 collective-permute-start.11
  22.1 0.5 collective-permute-done.9.refs_5_
  22.6 0.4 collective-permute-done.10.refs_6_
  23.0 0.2 collective-permute-done.11.refs_7_
  23.2 0.0 copy-done.9
  23.2 0.4 copy-done.10
  23.6 0.2 copy-done.11
  23.8 0.1 copy-done.3
  23.8 0.7 %copy-done.4 = f32[64,640]{1,0:T(8,128)} copy-done((f32[64,640]{1,0:T(8,128)}, f32[64,640]{1,0:T(8,128)S(1)}, u32[]{:S(2)}) %copy-start.4) | copy-done | bytes 163864
  24.5 13.4 %translate.1 = (f32[32,640]{1,0:T(8,128)}, f32[32,640]{1,0:T(8,128)}, f32[32,640]{1,0:T(8,128)}, f32[32,640]{1,0:T(8,128)}) custom-call(f32[32,640]{1,0:T(8,128)} %pack.1.c0, f32[32,640]{1,0:T(8,128)} %copy-done.2, f32[32,640]{1,0:T(8,128)} %copy-done.1, f32[32,640]{1,0:T(8,128)} %copy-done, f32[64,640]{1,0:T(8,128)} %copy-done.3, f32[64,640]{1,0:T(8,128)} %copy-done.4, ...), custom_call_target="tpu_custom_call" | custom-call | tf_op jit(solution)/shard_map/translate/pallas_call | solution.py:376
  37.9 3.6 %collective-permute-start.12 = (f32[32,640]{1,0:T(8,128)}, f32[32,640]{1,0:T(8,128)S(1)}, u32[]{:S(2)}, u32[]{:S(2)}) collective-permute-start(f32[32,640]{1,0:T(8,128)} %get-tuple-element.22), channel_id=1, source_target_pairs={{0,3},{1,2},{2,1},{3,0},{4,7},{5,6},{6,5},{7,4},{8,11},{9,10},{10,... | collective-permute-start | bytes 245768 | tf_op jit(solution)/shard_map/ppermute | solution.py:462
  41.5 0.8 %collective-permute-start.14 = (f32[32,640]{1,0:T(8,128)}, f32[32,640]{1,0:T(8,128)S(1)}, u32[]{:S(2)}, u32[]{:S(2)}) collective-permute-start(f32[32,640]{1,0:T(8,128)} %get-tuple-element.24), channel_id=1, source_target_pairs={{0,1},{1,0},{2,3},{3,2},{4,5},{5,4},{6,7},{7,6},{8,9},{9,8},{10,11... | collective-permute-start | bytes 245768 | tf_op jit(solution)/shard_map/ppermute | solution.py:462
  42.3 2.1 %collective-permute-done.12.p1 = f32[32,640]{1,0:T(8,128)S(1)} collective-permute-done((f32[32,640]{1,0:T(8,128)}, f32[32,640]{1,0:T(8,128)S(1)}, u32[]{:S(2)}, u32[]{:S(2)}) %collective-permute-start.12) | collective-permute-done | bytes 81952 | tf_op jit(solution)/shard_map/ppermute | solution.py:462
  44.4 5.1 %collective-permute-done.13.p2 = f32[32,640]{1,0:T(8,128)S(1)} collective-permute-done((f32[32,640]{1,0:T(8,128)}, f32[32,640]{1,0:T(8,128)S(1)}, u32[]{:S(2)}, u32[]{:S(2)}) %collective-permute-start.13) | collective-permute-done | bytes 81952 | tf_op jit(solution)/shard_map/ppermute | solution.py:462
  49.5 0.6 %copy-done.13 = f32[32,640]{1,0:T(8,128)} copy-done((f32[32,640]{1,0:T(8,128)}, f32[32,640]{1,0:T(8,128)S(1)}, u32[]{:S(2)}) %copy-start.13) | copy-done | bytes 81944
  50.2 1.9 %unpack.1 = f32[2,4,4,2,296]{4,3,2,1,0:T(2,128)} custom-call(s32[4,2,4]{2,1,0:T(2,128)} %bitcast.18, f32[32,640]{1,0:T(8,128)} %get-tuple-element.21.p0, f32[32,640]{1,0:T(8,128)} %copy-done.12, f32[32,640]{1,0:T(8,128)} %copy-done.13, f32[32,640]{1,0:T(8,128)} %copy-done.14), custom_call_target="tpu_custom_call" | custom-call | tf_op jit(solution)/shard_map/unpack/pallas_call | solution.py:153
  (37 shorter events, 0.1 us)
Async XLA Ops:
  1.8 11.3 %collective-permute-start.2 = (f32[32,640]{1,0:T(8,128)}, f32[32,640]{1,0:T(8,128)S(1)}, u32[]{:S(2)}, u32[]{:S(2)}) collective-permute-start(f32[32,640]{1,0:T(8,128)} %pack.1.c0), channel_id=1, source_target_pairs={{0,3},{1,2},{2,1},{3,0},{4,7},{5,6},{6,5},{7,4},{8,11},{9,10},{10,... | collective-permute-start | bytes 245768 | tf_op jit(solution)/shard_map/ppermute | solution.py:462
  6.9 7.1 %collective-permute-start.1 = (f32[32,640]{1,0:T(8,128)}, f32[32,640]{1,0:T(8,128)S(1)}, u32[]{:S(2)}, u32[]{:S(2)}) collective-permute-start(f32[32,640]{1,0:T(8,128)} %pack.1.c0), channel_id=1, source_target_pairs={{0,2},{1,3},{2,0},{3,1},{4,6},{5,7},{6,4},{7,5},{8,10},{9,11},{10,... | collective-permute-start | bytes 245768 | tf_op jit(solution)/shard_map/ppermute | solution.py:462
  6.9 7.1 %collective-permute-start = (f32[32,640]{1,0:T(8,128)}, f32[32,640]{1,0:T(8,128)S(1)}, u32[]{:S(2)}, u32[]{:S(2)}) collective-permute-start(f32[32,640]{1,0:T(8,128)} %pack.1.c0), channel_id=1, source_target_pairs={{0,1},{1,0},{2,3},{3,2},{4,5},{5,4},{6,7},{7,6},{8,9},{9,8},{10,11... | collective-permute-start | bytes 245768 | tf_op jit(solution)/shard_map/ppermute | solution.py:462
  9.1 6.2 %collective-permute-start.5 = (f32[240,128]{1,0:T(8,128)}, f32[240,128]{1,0:T(8,128)S(1)}, u32[]{:S(2)}, u32[]{:S(2)}) collective-permute-start(f32[240,128]{1,0:T(8,128)} %compact.1.refs_0_), channel_id=1, source_target_pairs={{0,24},{4,28},{8,16},{12,20},{16,8},{20,12},{24,0},{28,4},{1,25},{... | collective-permute-start | bytes 368648 | tf_op jit(solution)/shard_map/ppermute | solution.py:462
  11.9 5.6 %collective-permute-start.4 = (f32[240,128]{1,0:T(8,128)}, f32[240,128]{1,0:T(8,128)S(1)}, u32[]{:S(2)}, u32[]{:S(2)}) collective-permute-start(f32[240,128]{1,0:T(8,128)} %compact.1.refs_0_), channel_id=1, source_target_pairs={{0,16},{4,20},{8,24},{12,28},{16,0},{20,4},{24,8},{28,12},{1,17},{... | collective-permute-start | bytes 368648 | tf_op jit(solution)/shard_map/ppermute | solution.py:462
  13.2 10.0 %copy-start = (f32[32,640]{1,0:T(8,128)}, f32[32,640]{1,0:T(8,128)S(1)}, u32[]{:S(2)}) copy-start(f32[32,640]{1,0:T(8,128)S(1)} %collective-permute-done.2.c3) | copy-start | bytes 245764
  13.2 5.2 %collective-permute-start.3 = (f32[240,128]{1,0:T(8,128)}, f32[240,128]{1,0:T(8,128)S(1)}, u32[]{:S(2)}, u32[]{:S(2)}) collective-permute-start(f32[240,128]{1,0:T(8,128)} %compact.1.refs_0_), channel_id=1, source_target_pairs={{0,8},{4,12},{8,0},{12,4},{16,24},{20,28},{24,16},{28,20},{1,9},{5... | collective-permute-start | bytes 368648 | tf_op jit(solution)/shard_map/ppermute | solution.py:462
  14.0 9.2 %copy-start.1 = (f32[32,640]{1,0:T(8,128)}, f32[32,640]{1,0:T(8,128)S(1)}, u32[]{:S(2)}) copy-start(f32[32,640]{1,0:T(8,128)S(1)} %collective-permute-done.1.c2) | copy-start | bytes 245764
  14.0 9.2 %copy-start.2 = (f32[32,640]{1,0:T(8,128)}, f32[32,640]{1,0:T(8,128)S(1)}, u32[]{:S(2)}) copy-start(f32[32,640]{1,0:T(8,128)S(1)} %collective-permute-done.c1) | copy-start | bytes 245764
  15.3 7.8 %copy-start.5 = (f32[240,128]{1,0:T(8,128)}, f32[240,128]{1,0:T(8,128)S(1)}, u32[]{:S(2)}) copy-start(f32[240,128]{1,0:T(8,128)S(1)} %collective-permute-done.5.refs_3_) | copy-start | bytes 368644
  17.4 5.8 %copy-start.6 = (f32[240,128]{1,0:T(8,128)}, f32[240,128]{1,0:T(8,128)S(1)}, u32[]{:S(2)}) copy-start(f32[240,128]{1,0:T(8,128)S(1)} %collective-permute-done.4.refs_2_) | copy-start | bytes 368644
  18.3 4.9 %copy-start.7 = (f32[240,128]{1,0:T(8,128)}, f32[240,128]{1,0:T(8,128)S(1)}, u32[]{:S(2)}) copy-start(f32[240,128]{1,0:T(8,128)S(1)} %collective-permute-done.3.refs_1_) | copy-start | bytes 368644
  18.3 3.4 %collective-permute-start.8 = (f32[240,128]{1,0:T(8,128)}, f32[240,128]{1,0:T(8,128)S(1)}, u32[]{:S(2)}, u32[]{:S(2)}) collective-permute-start(f32[240,128]{1,0:T(8,128)} %compact.1.refs_0_), channel_id=1, source_target_pairs={{0,4},{4,0},{8,12},{12,8},{16,20},{20,16},{24,28},{28,24},{1,5},{5... | collective-permute-start | bytes 368648 | tf_op jit(solution)/shard_map/ppermute | solution.py:462
  18.3 4.8 %collective-permute-start.6 = (f32[64,640]{1,0:T(8,128)S(1)}, f32[64,640]{1,0:T(8,128)S(1)}, u32[]{:S(2)}, u32[]{:S(2)}) collective-permute-start(f32[64,640]{1,0:T(8,128)S(1)} %get-tuple-element.15), channel_id=1, source_target_pairs={{0,4},{4,0},{8,12},{12,8},{16,20},{20,16},{24,28},{28,24},{1,5},{5... | collective-permute-start | bytes 491528 | tf_op jit(solution)/shard_map/ppermute | solution.py:462
  18.8 4.3 %collective-permute-start.7 = (f32[64,640]{1,0:T(8,128)S(1)}, f32[64,640]{1,0:T(8,128)S(1)}, u32[]{:S(2)}, u32[]{:S(2)}) collective-permute-start(f32[64,640]{1,0:T(8,128)S(1)} %get-tuple-element.16), channel_id=1, source_target_pairs={{4,8},{12,16},{20,24},{8,4},{16,12},{24,20},{5,9},{13,17},{21,25},... | collective-permute-start | bytes 491528 | tf_op jit(solution)/shard_map/ppermute | solution.py:478
  19.5 3.1 %collective-permute-start.9 = (f32[240,128]{1,0:T(8,128)S(1)}, f32[240,128]{1,0:T(8,128)S(1)}, u32[]{:S(2)}, u32[]{:S(2)}) collective-permute-start(f32[240,128]{1,0:T(8,128)S(1)} %collective-permute-done.3.refs_1_), channel_id=1, source_target_pairs={{0,4},{4,0},{8,12},{12,8},{16,20},{20,16},{24,28},{28,24},{1,5},{5... | collective-permute-start | bytes 368648 | tf_op jit(solution)/shard_map/ppermute | solution.py:462
  21.6 1.3 %collective-permute-start.10 = (f32[240,128]{1,0:T(8,128)S(1)}, f32[240,128]{1,0:T(8,128)S(1)}, u32[]{:S(2)}, u32[]{:S(2)}) collective-permute-start(f32[240,128]{1,0:T(8,128)S(1)} %collective-permute-done.4.refs_2_), channel_id=1, source_target_pairs={{0,4},{4,0},{8,12},{12,8},{16,20},{20,16},{24,28},{28,24},{1,5},{5... | collective-permute-start | bytes 368648 | tf_op jit(solution)/shard_map/ppermute | solution.py:462
  21.7 1.5 %copy-start.8 = (f32[240,128]{1,0:T(8,128)}, f32[240,128]{1,0:T(8,128)S(1)}, u32[]{:S(2)}) copy-start(f32[240,128]{1,0:T(8,128)S(1)} %collective-permute-done.8.refs_4_) | copy-start | bytes 368644
  21.7 1.4 %collective-permute-start.11 = (f32[240,128]{1,0:T(8,128)S(1)}, f32[240,128]{1,0:T(8,128)S(1)}, u32[]{:S(2)}, u32[]{:S(2)}) collective-permute-start(f32[240,128]{1,0:T(8,128)S(1)} %collective-permute-done.5.refs_3_), channel_id=1, source_target_pairs={{0,4},{4,0},{8,12},{12,8},{16,20},{20,16},{24,28},{28,24},{1,5},{5... | collective-permute-start | bytes 368648 | tf_op jit(solution)/shard_map/ppermute | solution.py:462
  22.6 0.6 %copy-start.9 = (f32[240,128]{1,0:T(8,128)}, f32[240,128]{1,0:T(8,128)S(1)}, u32[]{:S(2)}) copy-start(f32[240,128]{1,0:T(8,128)S(1)} %collective-permute-done.9.refs_5_) | copy-start | bytes 368644
  23.0 0.7 %copy-start.10 = (f32[240,128]{1,0:T(8,128)}, f32[240,128]{1,0:T(8,128)S(1)}, u32[]{:S(2)}) copy-start(f32[240,128]{1,0:T(8,128)S(1)} %collective-permute-done.10.refs_6_) | copy-start | bytes 368644
  23.1 0.6 %copy-start.11 = (f32[240,128]{1,0:T(8,128)}, f32[240,128]{1,0:T(8,128)S(1)}, u32[]{:S(2)}) copy-start(f32[240,128]{1,0:T(8,128)S(1)} %collective-permute-done.11.refs_7_) | copy-start | bytes 368644
  23.1 0.7 %copy-start.3 = (f32[64,640]{1,0:T(8,128)}, f32[64,640]{1,0:T(8,128)S(1)}, u32[]{:S(2)}) copy-start(f32[64,640]{1,0:T(8,128)S(1)} %collective-permute-done.6.inner_ref) | copy-start | bytes 491524
  23.8 0.7 %copy-start.4 = (f32[64,640]{1,0:T(8,128)}, f32[64,640]{1,0:T(8,128)S(1)}, u32[]{:S(2)}) copy-start(f32[64,640]{1,0:T(8,128)S(1)} %collective-permute-done.7.outer_ref) | copy-start | bytes 491524
  37.9 6.5 %collective-permute-start.12 = (f32[32,640]{1,0:T(8,128)}, f32[32,640]{1,0:T(8,128)S(1)}, u32[]{:S(2)}, u32[]{:S(2)}) collective-permute-start(f32[32,640]{1,0:T(8,128)} %get-tuple-element.22), channel_id=1, source_target_pairs={{0,3},{1,2},{2,1},{3,0},{4,7},{5,6},{6,5},{7,4},{8,11},{9,10},{10,... | collective-permute-start | bytes 245768 | tf_op jit(solution)/shard_map/ppermute | solution.py:462
  41.5 8.0 %collective-permute-start.13 = (f32[32,640]{1,0:T(8,128)}, f32[32,640]{1,0:T(8,128)S(1)}, u32[]{:S(2)}, u32[]{:S(2)}) collective-permute-start(f32[32,640]{1,0:T(8,128)} %get-tuple-element.23), channel_id=1, source_target_pairs={{0,2},{1,3},{2,0},{3,1},{4,6},{5,7},{6,4},{7,5},{8,10},{9,11},{10,... | collective-permute-start | bytes 245768 | tf_op jit(solution)/shard_map/ppermute | solution.py:462
  41.5 8.0 %collective-permute-start.14 = (f32[32,640]{1,0:T(8,128)}, f32[32,640]{1,0:T(8,128)S(1)}, u32[]{:S(2)}, u32[]{:S(2)}) collective-permute-start(f32[32,640]{1,0:T(8,128)} %get-tuple-element.24), channel_id=1, source_target_pairs={{0,1},{1,0},{2,3},{3,2},{4,5},{5,4},{6,7},{7,6},{8,9},{9,8},{10,11... | collective-permute-start | bytes 245768 | tf_op jit(solution)/shard_map/ppermute | solution.py:462
  44.4 5.1 %copy-start.12 = (f32[32,640]{1,0:T(8,128)}, f32[32,640]{1,0:T(8,128)S(1)}, u32[]{:S(2)}) copy-start(f32[32,640]{1,0:T(8,128)S(1)} %collective-permute-done.12.p1) | copy-start | bytes 245764
  49.5 0.6 %copy-start.13 = (f32[32,640]{1,0:T(8,128)}, f32[32,640]{1,0:T(8,128)S(1)}, u32[]{:S(2)}) copy-start(f32[32,640]{1,0:T(8,128)S(1)} %collective-permute-done.13.p2) | copy-start | bytes 245764
  49.5 0.6 %copy-start.14 = (f32[32,640]{1,0:T(8,128)}, f32[32,640]{1,0:T(8,128)S(1)}, u32[]{:S(2)}) copy-start(f32[32,640]{1,0:T(8,128)S(1)} %collective-permute-done.14.p3) | copy-start | bytes 245764

commit v2 on v1

--- a/solution.py
+++ b/solution.py
@@ -199,11 +199,9 @@
         lanes = slice(place * LANES, (place + 1) * LANES)
         for at in range(0, 256, 32):
             rolled[at:at + 32, lanes] = pltpu.roll(rows[at:at + 32, lanes], 64, 1)
-    edge = jnp.zeros((54, LANES), jnp.float32)
-    for parent in range(4):
-        for place in (0, 9):
-            at = (parent * 10 + place) * 54
-            comps[at:at + 54, :] = edge
+    for at in range(0, comps.shape[0], 24):
+        comps[at:at + 8, :] = jnp.zeros((8, LANES), jnp.float32)
+        comps[at + 16:at + 24, :] = jnp.zeros((8, LANES), jnp.float32)
     total[...] = jnp.zeros_like(total)
 
     def split_store(ref, at, place, values):
@@ -262,8 +260,9 @@
                 left = left - piece.astype(jnp.float32)
                 pieces_in[block % 2, turn * KEPT_PADDED:turn * KEPT_PADDED + KEPT, lanes] = piece
         result = jnp.dot(matrix_ref[...], pieces_in[block % 2], preferred_element_type=jnp.float32)
-        for part in range(2):
-            kernel_ref[block, part] = result[:, part * LANES:(part + 1) * LANES]
+        k_re, k_im = result[:, :LANES], result[:, LANES:]
+        for part, value in enumerate((k_re, k_im - k_re, k_re + k_im)):
+            kernel_ref[block, part] = value
 
     def translate_block(block):
         for parent in range(4):
@@ -285,30 +284,35 @@
             for comp in range(27):
                 for part in range(2):
                     value = values[part, comp // 9, comp // 3 % 3, comp % 3]
-                    comps[pl.ds((parent * 10 + 1) * 54 + comp * 2 + part, 8, stride=54), :] = value
+                    at = ((comp * 4 + parent) * 2 + part) * 24 + 8
+                    comps[at:at + 8, :] = value
 
         def product(cx, cy, cz):
             comp = (cx * 3 + cy) * 3 + cz
-            have = [[None, None] for _ in range(2)]
+            have = [[None] * 3 for _ in range(2)]
             for ey in (-1, 0, 1):
                 source = []
                 for parent in range(4):
-                    at = (parent * 10 + 1 + ey) * 54 + comp * 2
-                    source.append([comps[pl.ds(at + part, 8, stride=54), :] for part in range(2)])
+                    at = (comp * 4 + parent) * 48 + 8 + ey
+                    s_re, s_im = (comps[at + 24 * part:at + 24 * part + 8, :] for part in range(2))
+                    source.append((s_re + s_im, s_re, s_im))
                 for place, (ex, neighbour_y) in enumerate(NEIGHBOURS):
                     if neighbour_y != ey:
                         continue
                     row = comp * 8 + place
-                    k_re, k_im = (
-                        jnp.broadcast_to(kernel_ref[block, part, row:row + 1, :], (8, LANES)) for part in range(2)
-                    )
+                    weights = [
+                        jnp.broadcast_to(kernel_ref[block, part, row:row + 1, :], (8, LANES)) for part in range(3)
+                    ]
                     for parent in range(2):
-                        s_re, s_im = source[parent + 1 + ex]
-                        terms = (k_re * s_re - k_im * s_im, k_re * s_im + k_im * s_re)
-                        for part in range(2):
+                        for part in range(3):
+                            term = weights[part] * source[parent + 1 + ex][part]
                             old = have[parent][part]
-                            have[parent][part] = terms[part] if old is None else old + terms[part]
-            return have[0] + have[1]
+                            have[parent][part] = term if old is None else old + term
+            found = []
+            for parent in range(2):
+                first, second, third = have[parent]
+                found += [first - third, first + second]
+            return found
 
         def merge(low, high, both):
             return [b + h for b, h in zip(both, high)] + [b + l for b, l in zip(both, low)]
@@ -382,14 +386,14 @@
             pltpu.VMEM((256, width), f32),
             pltpu.VMEM((class_blocks * 256, 768), bf16),
             pltpu.VMEM((2, block_count * 256, LANES), f32),
-            pltpu.VMEM((40 * 54, LANES), f32),
+            pltpu.VMEM((4 * 54 * 24, LANES), f32),
             pltpu.VMEM((2, 128, LANES), f32),
             pltpu.VMEM((block_count * 128, 768), bf16),
             pltpu.VMEM((class_blocks * 128, 256), f32),
             pltpu.VMEM((128, width), f32),
             pltpu.VMEM(tables.shape[1:], bf16),
             pltpu.VMEM((2, 3 * KEPT_PADDED, 2 * LANES), bf16),
-            pltpu.VMEM((block_count, 2, 27 * 8, LANES), f32),
+            pltpu.VMEM((block_count, 3, 27 * 8, LANES), f32),
             pltpu.SemaphoreType.DMA,
         ],
         out_shape=[jax.ShapeDtypeStruct((32, width), f32)] * 4,

time: 52.5 us -> 52 us (level)
  no operation moved by 1% of the time
where the time goes in v2:
time: 52 us; the launch traced here: 51.6 us
  Pallas kernels  18.3 us (35%)
  starting transfers between devices  17.5 us (34%)
  waiting for transfers between devices  12.9 us (25%)
  local copies, waits for them, and re-layouts  2.79 us (5%)
    ppermute x14, starting transfers between devices, exchange(): return lax.ppermute(values, axis, pairs)  16.8 us
    pallas_call x1, Pallas kernels, translate(): pl.pallas_call(functools.partial(translate_body, sub_count, freq_part), i...  12.9 us
    ppermute x14, waiting for transfers between devices, exchange(): return lax.ppermute(values, axis, pairs)  12.9 us
    unnamed x30, local copies, waits for them, and re-layouts  1.95 us
    pallas_call x1, Pallas kernels, unpack(): pl.pallas_call(unpack_body, in_specs=[pl.BlockSpec(memory_space=pltpu.VME...  1.87 us
    pallas_call x1, Pallas kernels, pack(): pl.pallas_call(pack_body, in_specs=[pl.BlockSpec(memory_space=pltpu.VMEM)...  1.84 us
    pallas_call x1, Pallas kernels, compact_kernels(): pl.pallas_call(compact_body, in_specs=[pl.BlockSpec(memory_space=pl.ANY)]...  1.65 us
  transfers between devices with their start and end apart: 15, of which 9 were waited for; matrix products, arithmetic and copies ran while one was open for 2% of the time, Pallas kernels for 3%

profile of v2, /device:TPU:0, one launch (start us, length us, event | category | flops | bytes accessed | tf_op | source)
XLA Modules:
  0.0 51.6 jit_solution(18305411754542839204)
XLA Ops:
  0.0 1.8 %pack.1.c0 = f32[32,640]{1,0:T(8,128)} custom-call(s32[4,2,4]{2,1,0:T(2,128)} %bitcast.17, f32[2,4,4,2,296]{4,3,2,1,0:T(2,128)} %density_ref.1), custom_call_target="tpu_custom_call" | custom-call | tf_op jit(solution)/shard_map/pack/pallas_call | solution.py:122
  1.8 5.0 %collective-permute-start.2 = (f32[32,640]{1,0:T(8,128)}, f32[32,640]{1,0:T(8,128)S(1)}, u32[]{:S(2)}, u32[]{:S(2)}) collective-permute-start(f32[32,640]{1,0:T(8,128)} %pack.1.c0), channel_id=1, source_target_pairs={{0,3},{1,2},{2,1},{3,0},{4,7},{5,6},{6,5},{7,4},{8,11},{9,10},{10,... | collective-permute-start | bytes 245768 | tf_op jit(solution)/shard_map/ppermute | solution.py:466
  6.9 0.6 %collective-permute-start = (f32[32,640]{1,0:T(8,128)}, f32[32,640]{1,0:T(8,128)S(1)}, u32[]{:S(2)}, u32[]{:S(2)}) collective-permute-start(f32[32,640]{1,0:T(8,128)} %pack.1.c0), channel_id=1, source_target_pairs={{0,1},{1,0},{2,3},{3,2},{4,5},{5,4},{6,7},{7,6},{8,9},{9,8},{10,11... | collective-permute-start | bytes 245768 | tf_op jit(solution)/shard_map/ppermute | solution.py:466
  7.5 1.7 %compact.1.refs_0_ = f32[240,128]{1,0:T(8,128)} custom-call(f32[632,128]{1,0:T(8,128)} %bitcast.16), custom_call_target="tpu_custom_call" | custom-call | tf_op jit(solution)/shard_map/compact/pallas_call | solution.py:76
  9.1 2.7 %collective-permute-start.5 = (f32[240,128]{1,0:T(8,128)}, f32[240,128]{1,0:T(8,128)S(1)}, u32[]{:S(2)}, u32[]{:S(2)}) collective-permute-start(f32[240,128]{1,0:T(8,128)} %compact.1.refs_0_), channel_id=1, source_target_pairs={{0,24},{4,28},{8,16},{12,20},{16,8},{20,12},{24,0},{28,4},{1,25},{... | collective-permute-start | bytes 368648 | tf_op jit(solution)/shard_map/ppermute | solution.py:466
  11.9 0.5 collective-permute-start.4
  12.4 0.8 %constant_dynamic-slice_fusion.3 = (f32[2,8,640]{2,1,0:T(8,128)S(1)}, f32[2,8,640]{2,1,0:T(8,128)S(1)}) fusion(f32[2,16,640]{2,1,0:T(8,128)} %bitcast.12, s32[]{:T(128)S(6)} %select_n.21, s32[]{:T(128)S(6)} %select_n.20), kind=kLoop, calls=%fused_computation.5 | loop fusion | bytes 163848 | tf_op jit(solution)/shard_map/dynamic_slice | solution.py:475
  13.2 0.4 collective-permute-start.3
  13.6 0.4 collective-permute-done.1.c2
  14.1 1.3 %collective-permute-done.5.refs_3_ = f32[240,128]{1,0:T(8,128)S(1)} collective-permute-done((f32[240,128]{1,0:T(8,128)}, f32[240,128]{1,0:T(8,128)S(1)}, u32[]{:S(2)}, u32[]{:S(2)}) %collective-permute-start.5) | collective-permute-done | bytes 122912 | tf_op jit(solution)/shard_map/ppermute | solution.py:466
  15.3 2.1 %collective-permute-done.4.refs_2_ = f32[240,128]{1,0:T(8,128)S(1)} collective-permute-done((f32[240,128]{1,0:T(8,128)}, f32[240,128]{1,0:T(8,128)S(1)}, u32[]{:S(2)}, u32[]{:S(2)}) %collective-permute-start.4) | collective-permute-done | bytes 122912 | tf_op jit(solution)/shard_map/ppermute | solution.py:466
  17.4 0.9 %collective-permute-done.3.refs_1_ = f32[240,128]{1,0:T(8,128)S(1)} collective-permute-done((f32[240,128]{1,0:T(8,128)}, f32[240,128]{1,0:T(8,128)S(1)}, u32[]{:S(2)}, u32[]{:S(2)}) %collective-permute-start.3) | collective-permute-done | bytes 122912 | tf_op jit(solution)/shard_map/ppermute | solution.py:466
  18.3 0.5 collective-permute-start.6
  18.8 0.7 %collective-permute-start.7 = (f32[64,640]{1,0:T(8,128)S(1)}, f32[64,640]{1,0:T(8,128)S(1)}, u32[]{:S(2)}, u32[]{:S(2)}) collective-permute-start(f32[64,640]{1,0:T(8,128)S(1)} %get-tuple-element.16), channel_id=1, source_target_pairs={{4,8},{12,16},{20,24},{8,4},{16,12},{24,20},{5,9},{13,17},{21,25},... | collective-permute-start | bytes 491528 | tf_op jit(solution)/shard_map/ppermute | solution.py:482
  19.5 2.1 %collective-permute-start.9 = (f32[240,128]{1,0:T(8,128)S(1)}, f32[240,128]{1,0:T(8,128)S(1)}, u32[]{:S(2)}, u32[]{:S(2)}) collective-permute-start(f32[240,128]{1,0:T(8,128)S(1)} %collective-permute-done.3.refs_1_), channel_id=1, source_target_pairs={{0,4},{4,0},{8,12},{12,8},{16,20},{20,16},{24,28},{28,24},{1,5},{5... | collective-permute-start | bytes 368648 | tf_op jit(solution)/shard_map/ppermute | solution.py:466
  21.6 0.1 collective-permute-start.10
  21.7 0.4 collective-permute-start.11
  22.1 0.5 collective-permute-done.9.refs_5_
  22.6 0.4 collective-permute-done.10.refs_6_
  23.0 0.2 collective-permute-done.11.refs_7_
  23.2 0.0 copy-done.9
  23.2 0.4 copy-done.10
  23.6 0.2 copy-done.11
  23.8 0.1 copy-done.3
  23.8 0.7 %copy-done.4 = f32[64,640]{1,0:T(8,128)} copy-done((f32[64,640]{1,0:T(8,128)}, f32[64,640]{1,0:T(8,128)S(1)}, u32[]{:S(2)}) %copy-start.4) | copy-done | bytes 163864
  24.5 12.9 %translate.1 = (f32[32,640]{1,0:T(8,128)}, f32[32,640]{1,0:T(8,128)}, f32[32,640]{1,0:T(8,128)}, f32[32,640]{1,0:T(8,128)}) custom-call(f32[32,640]{1,0:T(8,128)} %pack.1.c0, f32[32,640]{1,0:T(8,128)} %copy-done.2, f32[32,640]{1,0:T(8,128)} %copy-done.1, f32[32,640]{1,0:T(8,128)} %copy-done, f32[64,640]{1,0:T(8,128)} %copy-done.3, f32[64,640]{1,0:T(8,128)} %copy-done.4, ...), custom_call_target="tpu_custom_call" | custom-call | tf_op jit(solution)/shard_map/translate/pallas_call | solution.py:380
  37.4 3.6 %collective-permute-start.12 = (f32[32,640]{1,0:T(8,128)}, f32[32,640]{1,0:T(8,128)S(1)}, u32[]{:S(2)}, u32[]{:S(2)}) collective-permute-start(f32[32,640]{1,0:T(8,128)} %get-tuple-element.22), channel_id=1, source_target_pairs={{0,3},{1,2},{2,1},{3,0},{4,7},{5,6},{6,5},{7,4},{8,11},{9,10},{10,... | collective-permute-start | bytes 245768 | tf_op jit(solution)/shard_map/ppermute | solution.py:466
  41.0 0.8 %collective-permute-start.14 = (f32[32,640]{1,0:T(8,128)}, f32[32,640]{1,0:T(8,128)S(1)}, u32[]{:S(2)}, u32[]{:S(2)}) collective-permute-start(f32[32,640]{1,0:T(8,128)} %get-tuple-element.24), channel_id=1, source_target_pairs={{0,1},{1,0},{2,3},{3,2},{4,5},{5,4},{6,7},{7,6},{8,9},{9,8},{10,11... | collective-permute-start | bytes 245768 | tf_op jit(solution)/shard_map/ppermute | solution.py:466
  41.9 2.1 %collective-permute-done.12.p1 = f32[32,640]{1,0:T(8,128)S(1)} collective-permute-done((f32[32,640]{1,0:T(8,128)}, f32[32,640]{1,0:T(8,128)S(1)}, u32[]{:S(2)}, u32[]{:S(2)}) %collective-permute-start.12) | collective-permute-done | bytes 81952 | tf_op jit(solution)/shard_map/ppermute | solution.py:466
  43.9 5.1 %collective-permute-done.13.p2 = f32[32,640]{1,0:T(8,128)S(1)} collective-permute-done((f32[32,640]{1,0:T(8,128)}, f32[32,640]{1,0:T(8,128)S(1)}, u32[]{:S(2)}, u32[]{:S(2)}) %collective-permute-start.13) | collective-permute-done | bytes 81952 | tf_op jit(solution)/shard_map/ppermute | solution.py:466
  49.1 0.6 %copy-done.13 = f32[32,640]{1,0:T(8,128)} copy-done((f32[32,640]{1,0:T(8,128)}, f32[32,640]{1,0:T(8,128)S(1)}, u32[]{:S(2)}) %copy-start.13) | copy-done | bytes 81944
  49.7 1.9 %unpack.1 = f32[2,4,4,2,296]{4,3,2,1,0:T(2,128)} custom-call(s32[4,2,4]{2,1,0:T(2,128)} %bitcast.18, f32[32,640]{1,0:T(8,128)} %get-tuple-element.21.p0, f32[32,640]{1,0:T(8,128)} %copy-done.12, f32[32,640]{1,0:T(8,128)} %copy-done.13, f32[32,640]{1,0:T(8,128)} %copy-done.14), custom_call_target="tpu_custom_call" | custom-call | tf_op jit(solution)/shard_map/unpack/pallas_call | solution.py:153
  (37 shorter events, 0.1 us)
Async XLA Ops:
  1.8 11.3 %collective-permute-start.2 = (f32[32,640]{1,0:T(8,128)}, f32[32,640]{1,0:T(8,128)S(1)}, u32[]{:S(2)}, u32[]{:S(2)}) collective-permute-start(f32[32,640]{1,0:T(8,128)} %pack.1.c0), channel_id=1, source_target_pairs={{0,3},{1,2},{2,1},{3,0},{4,7},{5,6},{6,5},{7,4},{8,11},{9,10},{10,... | collective-permute-start | bytes 245768 | tf_op jit(solution)/shard_map/ppermute | solution.py:466
  6.9 7.1 %collective-permute-start.1 = (f32[32,640]{1,0:T(8,128)}, f32[32,640]{1,0:T(8,128)S(1)}, u32[]{:S(2)}, u32[]{:S(2)}) collective-permute-start(f32[32,640]{1,0:T(8,128)} %pack.1.c0), channel_id=1, source_target_pairs={{0,2},{1,3},{2,0},{3,1},{4,6},{5,7},{6,4},{7,5},{8,10},{9,11},{10,... | collective-permute-start | bytes 245768 | tf_op jit(solution)/shard_map/ppermute | solution.py:466
  6.9 7.1 %collective-permute-start = (f32[32,640]{1,0:T(8,128)}, f32[32,640]{1,0:T(8,128)S(1)}, u32[]{:S(2)}, u32[]{:S(2)}) collective-permute-start(f32[32,640]{1,0:T(8,128)} %pack.1.c0), channel_id=1, source_target_pairs={{0,1},{1,0},{2,3},{3,2},{4,5},{5,4},{6,7},{7,6},{8,9},{9,8},{10,11... | collective-permute-start | bytes 245768 | tf_op jit(solution)/shard_map/ppermute | solution.py:466
  9.1 6.2 %collective-permute-start.5 = (f32[240,128]{1,0:T(8,128)}, f32[240,128]{1,0:T(8,128)S(1)}, u32[]{:S(2)}, u32[]{:S(2)}) collective-permute-start(f32[240,128]{1,0:T(8,128)} %compact.1.refs_0_), channel_id=1, source_target_pairs={{0,24},{4,28},{8,16},{12,20},{16,8},{20,12},{24,0},{28,4},{1,25},{... | collective-permute-start | bytes 368648 | tf_op jit(solution)/shard_map/ppermute | solution.py:466
  11.9 5.6 %collective-permute-start.4 = (f32[240,128]{1,0:T(8,128)}, f32[240,128]{1,0:T(8,128)S(1)}, u32[]{:S(2)}, u32[]{:S(2)}) collective-permute-start(f32[240,128]{1,0:T(8,128)} %compact.1.refs_0_), channel_id=1, source_target_pairs={{0,16},{4,20},{8,24},{12,28},{16,0},{20,4},{24,8},{28,12},{1,17},{... | collective-permute-start | bytes 368648 | tf_op jit(solution)/shard_map/ppermute | solution.py:466
  13.2 10.0 %copy-start = (f32[32,640]{1,0:T(8,128)}, f32[32,640]{1,0:T(8,128)S(1)}, u32[]{:S(2)}) copy-start(f32[32,640]{1,0:T(8,128)S(1)} %collective-permute-done.2.c3) | copy-start | bytes 245764
  13.2 5.2 %collective-permute-start.3 = (f32[240,128]{1,0:T(8,128)}, f32[240,128]{1,0:T(8,128)S(1)}, u32[]{:S(2)}, u32[]{:S(2)}) collective-permute-start(f32[240,128]{1,0:T(8,128)} %compact.1.refs_0_), channel_id=1, source_target_pairs={{0,8},{4,12},{8,0},{12,4},{16,24},{20,28},{24,16},{28,20},{1,9},{5... | collective-permute-start | bytes 368648 | tf_op jit(solution)/shard_map/ppermute | solution.py:466
  14.0 9.2 %copy-start.1 = (f32[32,640]{1,0:T(8,128)}, f32[32,640]{1,0:T(8,128)S(1)}, u32[]{:S(2)}) copy-start(f32[32,640]{1,0:T(8,128)S(1)} %collective-permute-done.1.c2) | copy-start | bytes 245764
  14.0 9.2 %copy-start.2 = (f32[32,640]{1,0:T(8,128)}, f32[32,640]{1,0:T(8,128)S(1)}, u32[]{:S(2)}) copy-start(f32[32,640]{1,0:T(8,128)S(1)} %collective-permute-done.c1) | copy-start | bytes 245764
  15.3 7.8 %copy-start.5 = (f32[240,128]{1,0:T(8,128)}, f32[240,128]{1,0:T(8,128)S(1)}, u32[]{:S(2)}) copy-start(f32[240,128]{1,0:T(8,128)S(1)} %collective-permute-done.5.refs_3_) | copy-start | bytes 368644
  17.4 5.8 %copy-start.6 = (f32[240,128]{1,0:T(8,128)}, f32[240,128]{1,0:T(8,128)S(1)}, u32[]{:S(2)}) copy-start(f32[240,128]{1,0:T(8,128)S(1)} %collective-permute-done.4.refs_2_) | copy-start | bytes 368644
  18.3 4.9 %copy-start.7 = (f32[240,128]{1,0:T(8,128)}, f32[240,128]{1,0:T(8,128)S(1)}, u32[]{:S(2)}) copy-start(f32[240,128]{1,0:T(8,128)S(1)} %collective-permute-done.3.refs_1_) | copy-start | bytes 368644
  18.3 3.4 %collective-permute-start.8 = (f32[240,128]{1,0:T(8,128)}, f32[240,128]{1,0:T(8,128)S(1)}, u32[]{:S(2)}, u32[]{:S(2)}) collective-permute-start(f32[240,128]{1,0:T(8,128)} %compact.1.refs_0_), channel_id=1, source_target_pairs={{0,4},{4,0},{8,12},{12,8},{16,20},{20,16},{24,28},{28,24},{1,5},{5... | collective-permute-start | bytes 368648 | tf_op jit(solution)/shard_map/ppermute | solution.py:466
  18.3 4.8 %collective-permute-start.6 = (f32[64,640]{1,0:T(8,128)S(1)}, f32[64,640]{1,0:T(8,128)S(1)}, u32[]{:S(2)}, u32[]{:S(2)}) collective-permute-start(f32[64,640]{1,0:T(8,128)S(1)} %get-tuple-element.15), channel_id=1, source_target_pairs={{0,4},{4,0},{8,12},{12,8},{16,20},{20,16},{24,28},{28,24},{1,5},{5... | collective-permute-start | bytes 491528 | tf_op jit(solution)/shard_map/ppermute | solution.py:466
  18.8 4.3 %collective-permute-start.7 = (f32[64,640]{1,0:T(8,128)S(1)}, f32[64,640]{1,0:T(8,128)S(1)}, u32[]{:S(2)}, u32[]{:S(2)}) collective-permute-start(f32[64,640]{1,0:T(8,128)S(1)} %get-tuple-element.16), channel_id=1, source_target_pairs={{4,8},{12,16},{20,24},{8,4},{16,12},{24,20},{5,9},{13,17},{21,25},... | collective-permute-start | bytes 491528 | tf_op jit(solution)/shard_map/ppermute | solution.py:482
  19.5 3.1 %collective-permute-start.9 = (f32[240,128]{1,0:T(8,128)S(1)}, f32[240,128]{1,0:T(8,128)S(1)}, u32[]{:S(2)}, u32[]{:S(2)}) collective-permute-start(f32[240,128]{1,0:T(8,128)S(1)} %collective-permute-done.3.refs_1_), channel_id=1, source_target_pairs={{0,4},{4,0},{8,12},{12,8},{16,20},{20,16},{24,28},{28,24},{1,5},{5... | collective-permute-start | bytes 368648 | tf_op jit(solution)/shard_map/ppermute | solution.py:466
  21.6 1.3 %collective-permute-start.10 = (f32[240,128]{1,0:T(8,128)S(1)}, f32[240,128]{1,0:T(8,128)S(1)}, u32[]{:S(2)}, u32[]{:S(2)}) collective-permute-start(f32[240,128]{1,0:T(8,128)S(1)} %collective-permute-done.4.refs_2_), channel_id=1, source_target_pairs={{0,4},{4,0},{8,12},{12,8},{16,20},{20,16},{24,28},{28,24},{1,5},{5... | collective-permute-start | bytes 368648 | tf_op jit(solution)/shard_map/ppermute | solution.py:466
  21.7 1.5 %copy-start.8 = (f32[240,128]{1,0:T(8,128)}, f32[240,128]{1,0:T(8,128)S(1)}, u32[]{:S(2)}) copy-start(f32[240,128]{1,0:T(8,128)S(1)} %collective-permute-done.8.refs_4_) | copy-start | bytes 368644
  21.7 1.4 %collective-permute-start.11 = (f32[240,128]{1,0:T(8,128)S(1)}, f32[240,128]{1,0:T(8,128)S(1)}, u32[]{:S(2)}, u32[]{:S(2)}) collective-permute-start(f32[240,128]{1,0:T(8,128)S(1)} %collective-permute-done.5.refs_3_), channel_id=1, source_target_pairs={{0,4},{4,0},{8,12},{12,8},{16,20},{20,16},{24,28},{28,24},{1,5},{5... | collective-permute-start | bytes 368648 | tf_op jit(solution)/shard_map/ppermute | solution.py:466
  22.6 0.6 %copy-start.9 = (f32[240,128]{1,0:T(8,128)}, f32[240,128]{1,0:T(8,128)S(1)}, u32[]{:S(2)}) copy-start(f32[240,128]{1,0:T(8,128)S(1)} %collective-permute-done.9.refs_5_) | copy-start | bytes 368644
  23.0 0.7 %copy-start.10 = (f32[240,128]{1,0:T(8,128)}, f32[240,128]{1,0:T(8,128)S(1)}, u32[]{:S(2)}) copy-start(f32[240,128]{1,0:T(8,128)S(1)} %collective-permute-done.10.refs_6_) | copy-start | bytes 368644
  23.1 0.6 %copy-start.11 = (f32[240,128]{1,0:T(8,128)}, f32[240,128]{1,0:T(8,128)S(1)}, u32[]{:S(2)}) copy-start(f32[240,128]{1,0:T(8,128)S(1)} %collective-permute-done.11.refs_7_) | copy-start | bytes 368644
  23.1 0.7 %copy-start.3 = (f32[64,640]{1,0:T(8,128)}, f32[64,640]{1,0:T(8,128)S(1)}, u32[]{:S(2)}) copy-start(f32[64,640]{1,0:T(8,128)S(1)} %collective-permute-done.6.inner_ref) | copy-start | bytes 491524
  23.8 0.7 %copy-start.4 = (f32[64,640]{1,0:T(8,128)}, f32[64,640]{1,0:T(8,128)S(1)}, u32[]{:S(2)}) copy-start(f32[64,640]{1,0:T(8,128)S(1)} %collective-permute-done.7.outer_ref) | copy-start | bytes 491524
  37.4 6.5 %collective-permute-start.12 = (f32[32,640]{1,0:T(8,128)}, f32[32,640]{1,0:T(8,128)S(1)}, u32[]{:S(2)}, u32[]{:S(2)}) collective-permute-start(f32[32,640]{1,0:T(8,128)} %get-tuple-element.22), channel_id=1, source_target_pairs={{0,3},{1,2},{2,1},{3,0},{4,7},{5,6},{6,5},{7,4},{8,11},{9,10},{10,... | collective-permute-start | bytes 245768 | tf_op jit(solution)/shard_map/ppermute | solution.py:466
  41.0 8.0 %collective-permute-start.13 = (f32[32,640]{1,0:T(8,128)}, f32[32,640]{1,0:T(8,128)S(1)}, u32[]{:S(2)}, u32[]{:S(2)}) collective-permute-start(f32[32,640]{1,0:T(8,128)} %get-tuple-element.23), channel_id=1, source_target_pairs={{0,2},{1,3},{2,0},{3,1},{4,6},{5,7},{6,4},{7,5},{8,10},{9,11},{10,... | collective-permute-start | bytes 245768 | tf_op jit(solution)/shard_map/ppermute | solution.py:466
  41.0 8.0 %collective-permute-start.14 = (f32[32,640]{1,0:T(8,128)}, f32[32,640]{1,0:T(8,128)S(1)}, u32[]{:S(2)}, u32[]{:S(2)}) collective-permute-start(f32[32,640]{1,0:T(8,128)} %get-tuple-element.24), channel_id=1, source_target_pairs={{0,1},{1,0},{2,3},{3,2},{4,5},{5,4},{6,7},{7,6},{8,9},{9,8},{10,11... | collective-permute-start | bytes 245768 | tf_op jit(solution)/shard_map/ppermute | solution.py:466
  43.9 5.1 %copy-start.12 = (f32[32,640]{1,0:T(8,128)}, f32[32,640]{1,0:T(8,128)S(1)}, u32[]{:S(2)}) copy-start(f32[32,640]{1,0:T(8,128)S(1)} %collective-permute-done.12.p1) | copy-start | bytes 245764
  49.1 0.6 %copy-start.13 = (f32[32,640]{1,0:T(8,128)}, f32[32,640]{1,0:T(8,128)S(1)}, u32[]{:S(2)}) copy-start(f32[32,640]{1,0:T(8,128)S(1)} %collective-permute-done.13.p2) | copy-start | bytes 245764
  49.1 0.6 %copy-start.14 = (f32[32,640]{1,0:T(8,128)}, f32[32,640]{1,0:T(8,128)S(1)}, u32[]{:S(2)}) copy-start(f32[32,640]{1,0:T(8,128)S(1)} %collective-permute-done.14.p3) | copy-start | bytes 245764

commit v3 on v2

--- a/solution.py
+++ b/solution.py
@@ -478,11 +478,12 @@
     across = [(i, i + 1) for i in range(1, slab_count - 1, 2)]
     across += [(right, left) for left, right in across]
     outer, inner = rows_at(8 * core), rows_at(8 * (1 - core))
-    outer, inner, same_core = lax.optimization_barrier((outer, inner, same_core))
+    sibling = exchange(mine, "slab", 1)
+    _, _, same_core, sibling = lax.optimization_barrier((outer, inner, same_core, sibling))
     outer = lax.ppermute(outer, "slab", across)
     inner = exchange(inner, "slab", 1)
 
-    other_core = [exchange(block, "slab", 1) for block in same_core]
+    other_core = [sibling] + [exchange(block, "slab", 1) for block in same_core[1:]]
     pieces = LANES // freq_part
     block_count = slab_count // pieces
 

time: 52 us -> 49.4 us (0.950)
  starting transfers between devices: 17.5 us -> 16.2 us
  waiting for transfers between devices: 12.9 us -> 11.6 us
    ppermute x14, starting transfers between devices: 16.8 us -> 15.5 us  [exchange(): return lax.ppermute(values, axis, pairs)]
    ppermute x14, waiting for transfers between devices: 12.9 us -> 11.6 us  [exchange(): return lax.ppermute(values, axis, pairs)]
  transfers between devices with their start and end apart: 15 -> 15, of which waited for: 9 -> 8; matrix products, arithmetic and copies ran while one was open for 2% -> 2% of each run, Pallas kernels for 3% -> 3%
where the time goes in v3:
time: 49.4 us; the launch traced here: 49.1 us
  Pallas kernels  18.3 us (37%)
  starting transfers between devices  16.2 us (33%)
  waiting for transfers between devices  11.6 us (23%)
  local copies, waits for them, and re-layouts  2.8 us (6%)
    ppermute x14, starting transfers between devices, exchange(): return lax.ppermute(values, axis, pairs)  15.5 us
    pallas_call x1, Pallas kernels, translate(): pl.pallas_call(functools.partial(translate_body, sub_count, freq_part), i...  12.9 us
    ppermute x14, waiting for transfers between devices, exchange(): return lax.ppermute(values, axis, pairs)  11.6 us
    unnamed x30, local copies, waits for them, and re-layouts  1.97 us
    pallas_call x1, Pallas kernels, unpack(): pl.pallas_call(unpack_body, in_specs=[pl.BlockSpec(memory_space=pltpu.VME...  1.87 us
    pallas_call x1, Pallas kernels, pack(): pl.pallas_call(pack_body, in_specs=[pl.BlockSpec(memory_space=pltpu.VMEM)...  1.84 us
    pallas_call x1, Pallas kernels, compact_kernels(): pl.pallas_call(compact_body, in_specs=[pl.BlockSpec(memory_space=pl.ANY)]...  1.64 us
  transfers between devices with their start and end apart: 15, of which 8 were waited for; matrix products, arithmetic and copies ran while one was open for 2% of the time, Pallas kernels for 3%

profile of v3, /device:TPU:0, one launch (start us, length us, event | category | flops | bytes accessed | tf_op | source)
XLA Modules:
  0.0 49.1 jit_solution(14333301170285541163)
XLA Ops:
  0.0 1.8 %pack.1.c0 = f32[32,640]{1,0:T(8,128)} custom-call(s32[4,2,4]{2,1,0:T(2,128)} %bitcast.17, f32[2,4,4,2,296]{4,3,2,1,0:T(2,128)} %density_ref.1), custom_call_target="tpu_custom_call" | custom-call | tf_op jit(solution)/shard_map/pack/pallas_call | solution.py:122
  1.8 5.0 %collective-permute-start.2 = (f32[32,640]{1,0:T(8,128)}, f32[32,640]{1,0:T(8,128)S(1)}, u32[]{:S(2)}, u32[]{:S(2)}) collective-permute-start(f32[32,640]{1,0:T(8,128)} %pack.1.c0), channel_id=1, source_target_pairs={{0,3},{1,2},{2,1},{3,0},{4,7},{5,6},{6,5},{7,4},{8,11},{9,10},{10,... | collective-permute-start | bytes 245768 | tf_op jit(solution)/shard_map/ppermute | solution.py:466
  6.9 0.6 %collective-permute-start = (f32[32,640]{1,0:T(8,128)}, f32[32,640]{1,0:T(8,128)S(1)}, u32[]{:S(2)}, u32[]{:S(2)}) collective-permute-start(f32[32,640]{1,0:T(8,128)} %pack.1.c0), channel_id=1, source_target_pairs={{0,1},{1,0},{2,3},{3,2},{4,5},{5,4},{6,7},{7,6},{8,9},{9,8},{10,11... | collective-permute-start | bytes 245768 | tf_op jit(solution)/shard_map/ppermute | solution.py:466
  7.5 1.6 %compact.1.refs_0_ = f32[240,128]{1,0:T(8,128)} custom-call(f32[632,128]{1,0:T(8,128)} %bitcast.16), custom_call_target="tpu_custom_call" | custom-call | tf_op jit(solution)/shard_map/compact/pallas_call | solution.py:76
  9.1 0.1 collective-permute-start.8
  9.2 2.7 %collective-permute-start.7 = (f32[240,128]{1,0:T(8,128)}, f32[240,128]{1,0:T(8,128)S(1)}, u32[]{:S(2)}, u32[]{:S(2)}) collective-permute-start(f32[240,128]{1,0:T(8,128)} %compact.1.refs_0_), channel_id=1, source_target_pairs={{0,24},{4,28},{8,16},{12,20},{16,8},{20,12},{24,0},{28,4},{1,25},{... | collective-permute-start | bytes 368648 | tf_op jit(solution)/shard_map/ppermute | solution.py:466
  11.9 0.8 %constant_dynamic-slice_fusion.3 = (f32[2,8,640]{2,1,0:T(8,128)S(1)}, f32[2,8,640]{2,1,0:T(8,128)S(1)}) fusion(f32[2,16,640]{2,1,0:T(8,128)} %bitcast.12, s32[]{:T(128)S(6)} %select_n.21, s32[]{:T(128)S(6)} %select_n.20), kind=kLoop, calls=%fused_computation.5 | loop fusion | bytes 163848 | tf_op jit(solution)/shard_map/dynamic_slice | solution.py:475
  12.7 0.6 %collective-permute-start.6 = (f32[240,128]{1,0:T(8,128)}, f32[240,128]{1,0:T(8,128)S(1)}, u32[]{:S(2)}, u32[]{:S(2)}) collective-permute-start(f32[240,128]{1,0:T(8,128)} %compact.1.refs_0_), channel_id=1, source_target_pairs={{0,16},{4,20},{8,24},{12,28},{16,0},{20,4},{24,8},{28,12},{1,17},{... | collective-permute-start | bytes 368648 | tf_op jit(solution)/shard_map/ppermute | solution.py:466
  13.3 0.6 %collective-permute-done.1.c2 = f32[32,640]{1,0:T(8,128)S(1)} collective-permute-done((f32[32,640]{1,0:T(8,128)}, f32[32,640]{1,0:T(8,128)S(1)}, u32[]{:S(2)}, u32[]{:S(2)}) %collective-permute-start.1) | collective-permute-done | bytes 81952 | tf_op jit(solution)/shard_map/ppermute | solution.py:466
  14.0 1.5 %collective-permute-start.5 = (f32[240,128]{1,0:T(8,128)}, f32[240,128]{1,0:T(8,128)S(1)}, u32[]{:S(2)}, u32[]{:S(2)}) collective-permute-start(f32[240,128]{1,0:T(8,128)} %compact.1.refs_0_), channel_id=1, source_target_pairs={{0,8},{4,12},{8,0},{12,4},{16,24},{20,28},{24,16},{28,20},{1,9},{5... | collective-permute-start | bytes 368648 | tf_op jit(solution)/shard_map/ppermute | solution.py:466
  15.5 0.1 collective-permute-start.3
  15.6 0.7 %collective-permute-start.4 = (f32[64,640]{1,0:T(8,128)S(1)}, f32[64,640]{1,0:T(8,128)S(1)}, u32[]{:S(2)}, u32[]{:S(2)}) collective-permute-start(f32[64,640]{1,0:T(8,128)S(1)} %maximum_bitcast_fusion.1), channel_id=1, source_target_pairs={{4,8},{12,16},{20,24},{8,4},{16,12},{24,20},{5,9},{13,17},{21,25},... | collective-permute-start | bytes 491528 | tf_op jit(solution)/shard_map/ppermute | solution.py:483
  16.3 2.3 %collective-permute-done.6.refs_2_ = f32[240,128]{1,0:T(8,128)S(1)} collective-permute-done((f32[240,128]{1,0:T(8,128)}, f32[240,128]{1,0:T(8,128)S(1)}, u32[]{:S(2)}, u32[]{:S(2)}) %collective-permute-start.6) | collective-permute-done | bytes 122912 | tf_op jit(solution)/shard_map/ppermute | solution.py:466
  18.7 0.4 collective-permute-done.5.refs_1_
  19.1 0.5 %collective-permute-start.10 = (f32[240,128]{1,0:T(8,128)S(1)}, f32[240,128]{1,0:T(8,128)S(1)}, u32[]{:S(2)}, u32[]{:S(2)}) collective-permute-start(f32[240,128]{1,0:T(8,128)S(1)} %collective-permute-done.6.refs_2_), channel_id=1, source_target_pairs={{0,4},{4,0},{8,12},{12,8},{16,20},{20,16},{24,28},{28,24},{1,5},{5... | collective-permute-start | bytes 368648 | tf_op jit(solution)/shard_map/ppermute | solution.py:466
  19.6 0.0 collective-permute-start.11
  19.6 0.8 %collective-permute-done.9.refs_5_ = f32[240,128]{1,0:T(8,128)S(1)} collective-permute-done((f32[240,128]{1,0:T(8,128)S(1)}, f32[240,128]{1,0:T(8,128)S(1)}, u32[]{:S(2)}, u32[]{:S(2)}) %collective-permute-start.9) | collective-permute-done | bytes 122912 | tf_op jit(solution)/shard_map/ppermute | solution.py:466
  20.4 0.2 collective-permute-done.10.refs_6_
  20.6 0.3 collective-permute-done.11.refs_7_
  21.0 0.0 copy-done.9
  21.0 0.2 copy-done.10
  21.2 0.3 copy-done.11
  21.5 0.1 copy-done.3
  21.6 0.7 %copy-done.4 = f32[64,640]{1,0:T(8,128)} copy-done((f32[64,640]{1,0:T(8,128)}, f32[64,640]{1,0:T(8,128)S(1)}, u32[]{:S(2)}) %copy-start.4) | copy-done | bytes 163864
  22.3 12.9 %translate.1 = (f32[32,640]{1,0:T(8,128)}, f32[32,640]{1,0:T(8,128)}, f32[32,640]{1,0:T(8,128)}, f32[32,640]{1,0:T(8,128)}) custom-call(f32[32,640]{1,0:T(8,128)} %pack.1.c0, f32[32,640]{1,0:T(8,128)} %copy-done.2, f32[32,640]{1,0:T(8,128)} %copy-done.1, f32[32,640]{1,0:T(8,128)} %copy-done, f32[64,640]{1,0:T(8,128)} %copy-done.3, f32[64,640]{1,0:T(8,128)} %copy-done.4, ...), custom_call_target="tpu_custom_call" | custom-call | tf_op jit(solution)/shard_map/translate/pallas_call | solution.py:380
  35.2 3.6 %collective-permute-start.12 = (f32[32,640]{1,0:T(8,128)}, f32[32,640]{1,0:T(8,128)S(1)}, u32[]{:S(2)}, u32[]{:S(2)}) collective-permute-start(f32[32,640]{1,0:T(8,128)} %get-tuple-element.20), channel_id=1, source_target_pairs={{0,3},{1,2},{2,1},{3,0},{4,7},{5,6},{6,5},{7,4},{8,11},{9,10},{10,... | collective-permute-start | bytes 245768 | tf_op jit(solution)/shard_map/ppermute | solution.py:466
  38.8 0.9 %collective-permute-start.14 = (f32[32,640]{1,0:T(8,128)}, f32[32,640]{1,0:T(8,128)S(1)}, u32[]{:S(2)}, u32[]{:S(2)}) collective-permute-start(f32[32,640]{1,0:T(8,128)} %get-tuple-element.22), channel_id=1, source_target_pairs={{0,1},{1,0},{2,3},{3,2},{4,5},{5,4},{6,7},{7,6},{8,9},{9,8},{10,11... | collective-permute-start | bytes 245768 | tf_op jit(solution)/shard_map/ppermute | solution.py:466
  39.7 2.2 %collective-permute-done.12.p1 = f32[32,640]{1,0:T(8,128)S(1)} collective-permute-done((f32[32,640]{1,0:T(8,128)}, f32[32,640]{1,0:T(8,128)S(1)}, u32[]{:S(2)}, u32[]{:S(2)}) %collective-permute-start.12) | collective-permute-done | bytes 81952 | tf_op jit(solution)/shard_map/ppermute | solution.py:466
  41.8 4.8 %collective-permute-done.13.p2 = f32[32,640]{1,0:T(8,128)S(1)} collective-permute-done((f32[32,640]{1,0:T(8,128)}, f32[32,640]{1,0:T(8,128)S(1)}, u32[]{:S(2)}, u32[]{:S(2)}) %collective-permute-start.13) | collective-permute-done | bytes 81952 | tf_op jit(solution)/shard_map/ppermute | solution.py:466
  46.6 0.6 %copy-done.13 = f32[32,640]{1,0:T(8,128)} copy-done((f32[32,640]{1,0:T(8,128)}, f32[32,640]{1,0:T(8,128)S(1)}, u32[]{:S(2)}) %copy-start.13) | copy-done | bytes 81944
  47.2 0.0 copy-done.14
  47.2 1.9 %unpack.1 = f32[2,4,4,2,296]{4,3,2,1,0:T(2,128)} custom-call(s32[4,2,4]{2,1,0:T(2,128)} %bitcast.18, f32[32,640]{1,0:T(8,128)} %get-tuple-element.19.p0, f32[32,640]{1,0:T(8,128)} %copy-done.12, f32[32,640]{1,0:T(8,128)} %copy-done.13, f32[32,640]{1,0:T(8,128)} %copy-done.14), custom_call_target="tpu_custom_call" | custom-call | tf_op jit(solution)/shard_map/unpack/pallas_call | solution.py:153
  (38 shorter events, 0.1 us)
Async XLA Ops:
  1.8 10.9 %collective-permute-start.2 = (f32[32,640]{1,0:T(8,128)}, f32[32,640]{1,0:T(8,128)S(1)}, u32[]{:S(2)}, u32[]{:S(2)}) collective-permute-start(f32[32,640]{1,0:T(8,128)} %pack.1.c0), channel_id=1, source_target_pairs={{0,3},{1,2},{2,1},{3,0},{4,7},{5,6},{6,5},{7,4},{8,11},{9,10},{10,... | collective-permute-start | bytes 245768 | tf_op jit(solution)/shard_map/ppermute | solution.py:466
  6.9 7.1 %collective-permute-start.1 = (f32[32,640]{1,0:T(8,128)}, f32[32,640]{1,0:T(8,128)S(1)}, u32[]{:S(2)}, u32[]{:S(2)}) collective-permute-start(f32[32,640]{1,0:T(8,128)} %pack.1.c0), channel_id=1, source_target_pairs={{0,2},{1,3},{2,0},{3,1},{4,6},{5,7},{6,4},{7,5},{8,10},{9,11},{10,... | collective-permute-start | bytes 245768 | tf_op jit(solution)/shard_map/ppermute | solution.py:466
  6.9 8.6 %collective-permute-start = (f32[32,640]{1,0:T(8,128)}, f32[32,640]{1,0:T(8,128)S(1)}, u32[]{:S(2)}, u32[]{:S(2)}) collective-permute-start(f32[32,640]{1,0:T(8,128)} %pack.1.c0), channel_id=1, source_target_pairs={{0,1},{1,0},{2,3},{3,2},{4,5},{5,4},{6,7},{7,6},{8,9},{9,8},{10,11... | collective-permute-start | bytes 245768 | tf_op jit(solution)/shard_map/ppermute | solution.py:466
  9.1 6.5 %collective-permute-start.8 = (f32[240,128]{1,0:T(8,128)}, f32[240,128]{1,0:T(8,128)S(1)}, u32[]{:S(2)}, u32[]{:S(2)}) collective-permute-start(f32[240,128]{1,0:T(8,128)} %compact.1.refs_0_), channel_id=1, source_target_pairs={{0,4},{4,0},{8,12},{12,8},{16,20},{20,16},{24,28},{28,24},{1,5},{5... | collective-permute-start | bytes 368648 | tf_op jit(solution)/shard_map/ppermute | solution.py:466
  9.2 7.1 %collective-permute-start.7 = (f32[240,128]{1,0:T(8,128)}, f32[240,128]{1,0:T(8,128)S(1)}, u32[]{:S(2)}, u32[]{:S(2)}) collective-permute-start(f32[240,128]{1,0:T(8,128)} %compact.1.refs_0_), channel_id=1, source_target_pairs={{0,24},{4,28},{8,16},{12,20},{16,8},{20,12},{24,0},{28,4},{1,25},{... | collective-permute-start | bytes 368648 | tf_op jit(solution)/shard_map/ppermute | solution.py:466
  12.7 8.2 %copy-start = (f32[32,640]{1,0:T(8,128)}, f32[32,640]{1,0:T(8,128)S(1)}, u32[]{:S(2)}) copy-start(f32[32,640]{1,0:T(8,128)S(1)} %collective-permute-done.2.c3) | copy-start | bytes 245764
  12.7 5.9 %collective-permute-start.6 = (f32[240,128]{1,0:T(8,128)}, f32[240,128]{1,0:T(8,128)S(1)}, u32[]{:S(2)}, u32[]{:S(2)}) collective-permute-start(f32[240,128]{1,0:T(8,128)} %compact.1.refs_0_), channel_id=1, source_target_pairs={{0,16},{4,20},{8,24},{12,28},{16,0},{20,4},{24,8},{28,12},{1,17},{... | collective-permute-start | bytes 368648 | tf_op jit(solution)/shard_map/ppermute | solution.py:466
  14.0 7.0 %copy-start.1 = (f32[32,640]{1,0:T(8,128)}, f32[32,640]{1,0:T(8,128)S(1)}, u32[]{:S(2)}) copy-start(f32[32,640]{1,0:T(8,128)S(1)} %collective-permute-done.1.c2) | copy-start | bytes 245764
  14.0 5.1 %collective-permute-start.5 = (f32[240,128]{1,0:T(8,128)}, f32[240,128]{1,0:T(8,128)S(1)}, u32[]{:S(2)}, u32[]{:S(2)}) collective-permute-start(f32[240,128]{1,0:T(8,128)} %compact.1.refs_0_), channel_id=1, source_target_pairs={{0,8},{4,12},{8,0},{12,4},{16,24},{20,28},{24,16},{28,20},{1,9},{5... | collective-permute-start | bytes 368648 | tf_op jit(solution)/shard_map/ppermute | solution.py:466
  15.5 5.5 %copy-start.2 = (f32[32,640]{1,0:T(8,128)}, f32[32,640]{1,0:T(8,128)S(1)}, u32[]{:S(2)}) copy-start(f32[32,640]{1,0:T(8,128)S(1)} %collective-permute-done.c1) | copy-start | bytes 245764
  15.5 5.4 %collective-permute-start.3 = (f32[64,640]{1,0:T(8,128)S(1)}, f32[64,640]{1,0:T(8,128)S(1)}, u32[]{:S(2)}, u32[]{:S(2)}) collective-permute-start(f32[64,640]{1,0:T(8,128)S(1)} %maximum_bitcast_fusion), channel_id=1, source_target_pairs={{0,4},{4,0},{8,12},{12,8},{16,20},{20,16},{24,28},{28,24},{1,5},{5... | collective-permute-start | bytes 491528 | tf_op jit(solution)/shard_map/ppermute | solution.py:466
  15.6 5.3 %copy-start.5 = (f32[240,128]{1,0:T(8,128)}, f32[240,128]{1,0:T(8,128)S(1)}, u32[]{:S(2)}) copy-start(f32[240,128]{1,0:T(8,128)S(1)} %collective-permute-done.8.refs_4_) | copy-start | bytes 368644
  15.6 5.3 %collective-permute-start.4 = (f32[64,640]{1,0:T(8,128)S(1)}, f32[64,640]{1,0:T(8,128)S(1)}, u32[]{:S(2)}, u32[]{:S(2)}) collective-permute-start(f32[64,640]{1,0:T(8,128)S(1)} %maximum_bitcast_fusion.1), channel_id=1, source_target_pairs={{4,8},{12,16},{20,24},{8,4},{16,12},{24,20},{5,9},{13,17},{21,25},... | collective-permute-start | bytes 491528 | tf_op jit(solution)/shard_map/ppermute | solution.py:483
  16.3 4.6 %copy-start.6 = (f32[240,128]{1,0:T(8,128)}, f32[240,128]{1,0:T(8,128)S(1)}, u32[]{:S(2)}) copy-start(f32[240,128]{1,0:T(8,128)S(1)} %collective-permute-done.7.refs_3_) | copy-start | bytes 368644
  18.7 2.3 %copy-start.7 = (f32[240,128]{1,0:T(8,128)}, f32[240,128]{1,0:T(8,128)S(1)}, u32[]{:S(2)}) copy-start(f32[240,128]{1,0:T(8,128)S(1)} %collective-permute-done.6.refs_2_) | copy-start | bytes 368644
  19.1 1.9 %copy-start.8 = (f32[240,128]{1,0:T(8,128)}, f32[240,128]{1,0:T(8,128)S(1)}, u32[]{:S(2)}) copy-start(f32[240,128]{1,0:T(8,128)S(1)} %collective-permute-done.5.refs_1_) | copy-start | bytes 368644
  19.1 1.3 %collective-permute-start.9 = (f32[240,128]{1,0:T(8,128)S(1)}, f32[240,128]{1,0:T(8,128)S(1)}, u32[]{:S(2)}, u32[]{:S(2)}) collective-permute-start(f32[240,128]{1,0:T(8,128)S(1)} %collective-permute-done.5.refs_1_), channel_id=1, source_target_pairs={{0,4},{4,0},{8,12},{12,8},{16,20},{20,16},{24,28},{28,24},{1,5},{5... | collective-permute-start | bytes 368648 | tf_op jit(solution)/shard_map/ppermute | solution.py:466
  19.1 1.5 %collective-permute-start.10 = (f32[240,128]{1,0:T(8,128)S(1)}, f32[240,128]{1,0:T(8,128)S(1)}, u32[]{:S(2)}, u32[]{:S(2)}) collective-permute-start(f32[240,128]{1,0:T(8,128)S(1)} %collective-permute-done.6.refs_2_), channel_id=1, source_target_pairs={{0,4},{4,0},{8,12},{12,8},{16,20},{20,16},{24,28},{28,24},{1,5},{5... | collective-permute-start | bytes 368648 | tf_op jit(solution)/shard_map/ppermute | solution.py:466
  19.6 1.3 %collective-permute-start.11 = (f32[240,128]{1,0:T(8,128)S(1)}, f32[240,128]{1,0:T(8,128)S(1)}, u32[]{:S(2)}, u32[]{:S(2)}) collective-permute-start(f32[240,128]{1,0:T(8,128)S(1)} %collective-permute-done.7.refs_3_), channel_id=1, source_target_pairs={{0,4},{4,0},{8,12},{12,8},{16,20},{20,16},{24,28},{28,24},{1,5},{5... | collective-permute-start | bytes 368648 | tf_op jit(solution)/shard_map/ppermute | solution.py:466
  20.4 0.6 %copy-start.9 = (f32[240,128]{1,0:T(8,128)}, f32[240,128]{1,0:T(8,128)S(1)}, u32[]{:S(2)}) copy-start(f32[240,128]{1,0:T(8,128)S(1)} %collective-permute-done.9.refs_5_) | copy-start | bytes 368644
  20.6 0.7 %copy-start.10 = (f32[240,128]{1,0:T(8,128)}, f32[240,128]{1,0:T(8,128)S(1)}, u32[]{:S(2)}) copy-start(f32[240,128]{1,0:T(8,128)S(1)} %collective-permute-done.10.refs_6_) | copy-start | bytes 368644
  20.9 0.6 %copy-start.11 = (f32[240,128]{1,0:T(8,128)}, f32[240,128]{1,0:T(8,128)S(1)}, u32[]{:S(2)}) copy-start(f32[240,128]{1,0:T(8,128)S(1)} %collective-permute-done.11.refs_7_) | copy-start | bytes 368644
  20.9 0.7 %copy-start.3 = (f32[64,640]{1,0:T(8,128)}, f32[64,640]{1,0:T(8,128)S(1)}, u32[]{:S(2)}) copy-start(f32[64,640]{1,0:T(8,128)S(1)} %collective-permute-done.3.inner_ref) | copy-start | bytes 491524
  21.6 0.7 %copy-start.4 = (f32[64,640]{1,0:T(8,128)}, f32[64,640]{1,0:T(8,128)S(1)}, u32[]{:S(2)}) copy-start(f32[64,640]{1,0:T(8,128)S(1)} %collective-permute-done.4.outer_ref) | copy-start | bytes 491524
  35.2 6.6 %collective-permute-start.12 = (f32[32,640]{1,0:T(8,128)}, f32[32,640]{1,0:T(8,128)S(1)}, u32[]{:S(2)}, u32[]{:S(2)}) collective-permute-start(f32[32,640]{1,0:T(8,128)} %get-tuple-element.20), channel_id=1, source_target_pairs={{0,3},{1,2},{2,1},{3,0},{4,7},{5,6},{6,5},{7,4},{8,11},{9,10},{10,... | collective-permute-start | bytes 245768 | tf_op jit(solution)/shard_map/ppermute | solution.py:466
  38.8 7.8 %collective-permute-start.13 = (f32[32,640]{1,0:T(8,128)}, f32[32,640]{1,0:T(8,128)S(1)}, u32[]{:S(2)}, u32[]{:S(2)}) collective-permute-start(f32[32,640]{1,0:T(8,128)} %get-tuple-element.21), channel_id=1, source_target_pairs={{0,2},{1,3},{2,0},{3,1},{4,6},{5,7},{6,4},{7,5},{8,10},{9,11},{10,... | collective-permute-start | bytes 245768 | tf_op jit(solution)/shard_map/ppermute | solution.py:466
  38.8 7.8 %collective-permute-start.14 = (f32[32,640]{1,0:T(8,128)}, f32[32,640]{1,0:T(8,128)S(1)}, u32[]{:S(2)}, u32[]{:S(2)}) collective-permute-start(f32[32,640]{1,0:T(8,128)} %get-tuple-element.22), channel_id=1, source_target_pairs={{0,1},{1,0},{2,3},{3,2},{4,5},{5,4},{6,7},{7,6},{8,9},{9,8},{10,11... | collective-permute-start | bytes 245768 | tf_op jit(solution)/shard_map/ppermute | solution.py:466
  41.8 4.8 %copy-start.12 = (f32[32,640]{1,0:T(8,128)}, f32[32,640]{1,0:T(8,128)S(1)}, u32[]{:S(2)}) copy-start(f32[32,640]{1,0:T(8,128)S(1)} %collective-permute-done.12.p1) | copy-start | bytes 245764
  46.6 0.6 %copy-start.13 = (f32[32,640]{1,0:T(8,128)}, f32[32,640]{1,0:T(8,128)S(1)}, u32[]{:S(2)}) copy-start(f32[32,640]{1,0:T(8,128)S(1)} %collective-permute-done.13.p2) | copy-start | bytes 245764
  46.6 0.6 %copy-start.14 = (f32[32,640]{1,0:T(8,128)}, f32[32,640]{1,0:T(8,128)S(1)}, u32[]{:S(2)}) copy-start(f32[32,640]{1,0:T(8,128)S(1)} %collective-permute-done.14.p3) | copy-start | bytes 245764

commit v4 on v3

--- a/solution.py
+++ b/solution.py
@@ -62,27 +62,6 @@
     return found
 
 
-def compact_body(kernel_ref, out_ref, held, sem):
-    copy = pltpu.make_async_copy(kernel_ref, held, sem)
-    copy.start()
-    copy.wait()
-    for key, slot in GROUPS.items():
-        row = 2 * GROUP_ROW[key]
-        out_ref[row:row + 6, :] = held[2 * slot:2 * slot + 6, :]
-
-
-def compact_kernels(kernels):
-    rows, width = kernels.shape[1:]
-    return pl.pallas_call(
-        compact_body,
-        in_specs=[pl.BlockSpec(memory_space=pl.ANY)],
-        out_specs=pl.BlockSpec(memory_space=pltpu.VMEM),
-        out_shape=jax.ShapeDtypeStruct((2 * KEPT, width), jnp.float32),
-        scratch_shapes=[pltpu.VMEM((2 * rows, width), jnp.float32), pltpu.SemaphoreType.DMA],
-        name="compact",
-    )(kernels.transpose(1, 0, 2).reshape(2 * rows, width))
-
-
 def row_of(x, y, z):
     return (y // 2) * 16 + x * 4 + z * 2 + y % 2
 
@@ -91,14 +70,21 @@
     return 64 + 28 * (x - 1)
 
 
-def pack_body(occupied_ref, density_ref, out_ref, rows_re, rows_im):
+def prepare_body(occupied_ref, density_ref, kernel_ref, own_ref, kept_ref, density, kernels, rows_re, rows_im, sems):
+    copies = [
+        pltpu.make_async_copy(density_ref, density, sems.at[0]),
+        pltpu.make_async_copy(kernel_ref, kernels, sems.at[1]),
+    ]
+    for copy in copies:
+        copy.start()
+    copies[0].wait()
     for x in range(4):
         for y in range(4):
             for z in range(2):
                 keep = occupied_ref[x, z:z + 1, y:y + 1] > 0
                 row = row_of(x, y, z)
                 for part, rows in enumerate((rows_re, rows_im)):
-                    values = density_ref[part, x, y, z:z + 1, :]
+                    values = density[part, x, y, z:z + 1, :]
                     rows[row:row + 1, :] = jnp.where(keep, values, 0.0)
     parts = (rows_re[...], rows_im[...])
     gap = jnp.zeros((32, 4), jnp.float32)
@@ -114,19 +100,36 @@
                 pieces += [part[:, at:at + 28], gap]
         columns.append(pieces)
     for place, pieces in enumerate(columns):
-        out_ref[:, place * LANES:(place + 1) * LANES] = jnp.concatenate(pieces, axis=1)
-
-
-def pack(occupied, density):
-    width = density.shape[-1]
+        own_ref[:, place * LANES:(place + 1) * LANES] = jnp.concatenate(pieces, axis=1)
+    copies[1].wait()
+    for key, slot in GROUPS.items():
+        row = 2 * GROUP_ROW[key]
+        kept_ref[row:row + 6, :] = kernels[2 * slot:2 * slot + 6, :]
+
+
+def prepare(occupied, density, kernels):
+    rows, width = 2 * kernels.shape[1], kernels.shape[2]
+    surf_count = density.shape[-1]
+    f32 = jnp.float32
+    in_vmem = pl.BlockSpec(memory_space=pltpu.VMEM)
+    anywhere = pl.BlockSpec(memory_space=pl.ANY)
     return pl.pallas_call(
-        pack_body,
-        in_specs=[pl.BlockSpec(memory_space=pltpu.VMEM), pl.BlockSpec(memory_space=pltpu.VMEM)],
-        out_specs=pl.BlockSpec(memory_space=pltpu.VMEM),
-        out_shape=jax.ShapeDtypeStruct((32, COLUMNS * LANES), jnp.float32),
-        scratch_shapes=[pltpu.VMEM((32, width), jnp.float32)] * 2,
-        name="pack",
-    )(occupied.transpose(0, 2, 1), density)
+        prepare_body,
+        in_specs=[in_vmem, anywhere, anywhere],
+        out_specs=[in_vmem] * 2,
+        out_shape=[
+            jax.ShapeDtypeStruct((32, COLUMNS * LANES), f32),
+            jax.ShapeDtypeStruct((2 * KEPT, width), f32),
+        ],
+        scratch_shapes=[
+            pltpu.VMEM(density.shape, f32),
+            pltpu.VMEM((rows, width), f32),
+            pltpu.VMEM((32, surf_count), f32),
+            pltpu.VMEM((32, surf_count), f32),
+            pltpu.SemaphoreType.DMA((2,)),
+        ],
+        name="prepare",
+    )(occupied.transpose(0, 2, 1), density, kernels.transpose(1, 0, 2).reshape(rows, width))
 
 
 def unpack_body(occupied_ref, p0, p1, p2, p3, out_ref, rows_re, rows_im):
@@ -465,7 +468,7 @@
         pairs = [(i, i ^ bits) for i in range(lax.axis_size(axis))]
         return lax.ppermute(values, axis, pairs)
 
-    own, mine = pack(occupied, density), compact_kernels(kernels)
+    own, mine = prepare(occupied, density, kernels)
     width = own.shape[-1]
     chunks = [own] + [exchange(own, "sub", k) for k in range(1, 4)]
 

time: 49.4 us -> 50.5 us (1.022)
  waiting for transfers between devices: 11.6 us -> 13.3 us
  Pallas kernels: 18.3 us -> 17.4 us
    ppermute x14, waiting for transfers between devices: 11.6 us -> 13.3 us  [exchange(): return lax.ppermute(values, axis, pairs)]
    pallas_call x2 -> x1, Pallas kernels: 3.48 us -> 2.58 us  [prepare(): pl.pallas_call(prepare_body, in_specs=[in_vmem, anywhere, anywhere], out_...]
  transfers between devices with their start and end apart: 15 -> 15, of which waited for: 8 -> 8; matrix products, arithmetic and copies ran while one was open for 2% -> 2% of each run, Pallas kernels for 3% -> 0%
where the time goes in v4:
time: 50.5 us; the launch traced here: 50.2 us
  Pallas kernels  17.4 us (34%)
  starting transfers between devices  16.5 us (33%)
  waiting for transfers between devices  13.3 us (26%)
  local copies, waits for them, and re-layouts  2.78 us (6%)
    ppermute x14, starting transfers between devices, exchange(): return lax.ppermute(values, axis, pairs)  15.8 us
    ppermute x14, waiting for transfers between devices, exchange(): return lax.ppermute(values, axis, pairs)  13.3 us
    pallas_call x1, Pallas kernels, translate(): pl.pallas_call(functools.partial(translate_body, sub_count, freq_part), i...  12.9 us
    pallas_call x1, Pallas kernels, prepare(): pl.pallas_call(prepare_body, in_specs=[in_vmem, anywhere, anywhere], out_...  2.58 us
    unnamed x30, local copies, waits for them, and re-layouts  1.95 us
    pallas_call x1, Pallas kernels, unpack(): pl.pallas_call(unpack_body, in_specs=[pl.BlockSpec(memory_space=pltpu.VME...  1.87 us
  transfers between devices with their start and end apart: 15, of which 8 were waited for; matrix products, arithmetic and copies ran while one was open for 2% of the time, Pallas kernels for 0%

profile of v4, /device:TPU:0, one launch (start us, length us, event | category | flops | bytes accessed | tf_op | source)
XLA Modules:
  0.0 50.2 jit_solution(5215205128575742600)
XLA Ops:
  0.0 2.6 %prepare.1 = (f32[32,640]{1,0:T(8,128)}, f32[240,128]{1,0:T(8,128)}) custom-call(s32[4,2,4]{2,1,0:T(2,128)} %bitcast.17, f32[2,4,4,2,296]{4,3,2,1,0:T(2,128)} %density_ref.1, f32[632,128]{1,0:T(8,128)} %bitcast.16), custom_call_target="tpu_custom_call" | custom-call | tf_op jit(solution)/shard_map/prepare/pallas_call | solution.py:116
  2.6 5.1 %collective-permute-start.2 = (f32[32,640]{1,0:T(8,128)}, f32[32,640]{1,0:T(8,128)S(1)}, u32[]{:S(2)}, u32[]{:S(2)}) collective-permute-start(f32[32,640]{1,0:T(8,128)} %get-tuple-element.16.c0), channel_id=1, source_target_pairs={{0,3},{1,2},{2,1},{3,0},{4,7},{5,6},{6,5},{7,4},{8,11},{9,10},{10,... | collective-permute-start | bytes 245768 | tf_op jit(solution)/shard_map/ppermute | solution.py:469
  7.7 0.0 collective-permute-start.1
  7.7 0.6 %collective-permute-start = (f32[32,640]{1,0:T(8,128)}, f32[32,640]{1,0:T(8,128)S(1)}, u32[]{:S(2)}, u32[]{:S(2)}) collective-permute-start(f32[32,640]{1,0:T(8,128)} %get-tuple-element.16.c0), channel_id=1, source_target_pairs={{0,1},{1,0},{2,3},{3,2},{4,5},{5,4},{6,7},{7,6},{8,9},{9,8},{10,11... | collective-permute-start | bytes 245768 | tf_op jit(solution)/shard_map/ppermute | solution.py:469
  8.3 0.0 collective-permute-start.8
  8.4 2.6 %collective-permute-start.7 = (f32[240,128]{1,0:T(8,128)}, f32[240,128]{1,0:T(8,128)S(1)}, u32[]{:S(2)}, u32[]{:S(2)}) collective-permute-start(f32[240,128]{1,0:T(8,128)} %get-tuple-element.18.refs_0_), channel_id=1, source_target_pairs={{0,24},{4,28},{8,16},{12,20},{16,8},{20,12},{24,0},{28,4},{1,25},{... | collective-permute-start | bytes 368648 | tf_op jit(solution)/shard_map/ppermute | solution.py:469
  10.9 0.8 %constant_dynamic-slice_fusion.3 = (f32[2,8,640]{2,1,0:T(8,128)S(1)}, f32[2,8,640]{2,1,0:T(8,128)S(1)}) fusion(f32[2,16,640]{2,1,0:T(8,128)} %bitcast.12, s32[]{:T(128)S(6)} %select_n.21, s32[]{:T(128)S(6)} %select_n.20), kind=kLoop, calls=%fused_computation.5 | loop fusion | bytes 163848 | tf_op jit(solution)/shard_map/dynamic_slice | solution.py:478
  11.8 1.0 %collective-permute-start.6 = (f32[240,128]{1,0:T(8,128)}, f32[240,128]{1,0:T(8,128)S(1)}, u32[]{:S(2)}, u32[]{:S(2)}) collective-permute-start(f32[240,128]{1,0:T(8,128)} %get-tuple-element.18.refs_0_), channel_id=1, source_target_pairs={{0,16},{4,20},{8,24},{12,28},{16,0},{20,4},{24,8},{28,12},{1,17},{... | collective-permute-start | bytes 368648 | tf_op jit(solution)/shard_map/ppermute | solution.py:469
  12.7 2.0 %collective-permute-done.1.c2 = f32[32,640]{1,0:T(8,128)S(1)} collective-permute-done((f32[32,640]{1,0:T(8,128)}, f32[32,640]{1,0:T(8,128)S(1)}, u32[]{:S(2)}, u32[]{:S(2)}) %collective-permute-start.1) | collective-permute-done | bytes 81952 | tf_op jit(solution)/shard_map/ppermute | solution.py:469
  14.8 1.5 %collective-permute-start.5 = (f32[240,128]{1,0:T(8,128)}, f32[240,128]{1,0:T(8,128)S(1)}, u32[]{:S(2)}, u32[]{:S(2)}) collective-permute-start(f32[240,128]{1,0:T(8,128)} %get-tuple-element.18.refs_0_), channel_id=1, source_target_pairs={{0,8},{4,12},{8,0},{12,4},{16,24},{20,28},{24,16},{28,20},{1,9},{5... | collective-permute-start | bytes 368648 | tf_op jit(solution)/shard_map/ppermute | solution.py:469
  16.3 0.1 collective-permute-start.3
  16.5 0.7 %collective-permute-start.4 = (f32[64,640]{1,0:T(8,128)S(1)}, f32[64,640]{1,0:T(8,128)S(1)}, u32[]{:S(2)}, u32[]{:S(2)}) collective-permute-start(f32[64,640]{1,0:T(8,128)S(1)} %maximum_bitcast_fusion.1), channel_id=1, source_target_pairs={{4,8},{12,16},{20,24},{8,4},{16,12},{24,20},{5,9},{13,17},{21,25},... | collective-permute-start | bytes 491528 | tf_op jit(solution)/shard_map/ppermute | solution.py:486
  17.2 0.7 %collective-permute-done.6.refs_2_ = f32[240,128]{1,0:T(8,128)S(1)} collective-permute-done((f32[240,128]{1,0:T(8,128)}, f32[240,128]{1,0:T(8,128)S(1)}, u32[]{:S(2)}, u32[]{:S(2)}) %collective-permute-start.6) | collective-permute-done | bytes 122912 | tf_op jit(solution)/shard_map/ppermute | solution.py:469
  17.8 2.0 %collective-permute-done.5.refs_1_ = f32[240,128]{1,0:T(8,128)S(1)} collective-permute-done((f32[240,128]{1,0:T(8,128)}, f32[240,128]{1,0:T(8,128)S(1)}, u32[]{:S(2)}, u32[]{:S(2)}) %collective-permute-start.5) | collective-permute-done | bytes 122912 | tf_op jit(solution)/shard_map/ppermute | solution.py:469
  19.9 0.5 %collective-permute-start.10 = (f32[240,128]{1,0:T(8,128)S(1)}, f32[240,128]{1,0:T(8,128)S(1)}, u32[]{:S(2)}, u32[]{:S(2)}) collective-permute-start(f32[240,128]{1,0:T(8,128)S(1)} %collective-permute-done.6.refs_2_), channel_id=1, source_target_pairs={{0,4},{4,0},{8,12},{12,8},{16,20},{20,16},{24,28},{28,24},{1,5},{5... | collective-permute-start | bytes 368648 | tf_op jit(solution)/shard_map/ppermute | solution.py:469
  20.4 0.0 collective-permute-start.11
  20.4 0.8 %collective-permute-done.9.refs_5_ = f32[240,128]{1,0:T(8,128)S(1)} collective-permute-done((f32[240,128]{1,0:T(8,128)S(1)}, f32[240,128]{1,0:T(8,128)S(1)}, u32[]{:S(2)}, u32[]{:S(2)}) %collective-permute-start.9) | collective-permute-done | bytes 122912 | tf_op jit(solution)/shard_map/ppermute | solution.py:469
  21.2 0.2 collective-permute-done.10.refs_6_
  21.4 0.3 collective-permute-done.11.refs_7_
  21.8 0.0 copy-done.9
  21.9 0.2 copy-done.10
  22.0 0.3 copy-done.11
  22.4 0.1 copy-done.3
  22.4 0.7 %copy-done.4 = f32[64,640]{1,0:T(8,128)} copy-done((f32[64,640]{1,0:T(8,128)}, f32[64,640]{1,0:T(8,128)S(1)}, u32[]{:S(2)}) %copy-start.4) | copy-done | bytes 163864
  23.1 12.9 %translate.1 = (f32[32,640]{1,0:T(8,128)}, f32[32,640]{1,0:T(8,128)}, f32[32,640]{1,0:T(8,128)}, f32[32,640]{1,0:T(8,128)}) custom-call(f32[32,640]{1,0:T(8,128)} %get-tuple-element.16.c0, f32[32,640]{1,0:T(8,128)} %copy-done.2, f32[32,640]{1,0:T(8,128)} %copy-done.1, f32[32,640]{1,0:T(8,128)} %copy-done, f32[64,640]{1,0:T(8,128)} %copy-done.3, ...), custom_call_target="tpu_custom_call" | custom-call | tf_op jit(solution)/shard_map/translate/pallas_call | solution.py:383
  36.0 2.8 %collective-permute-start.12 = (f32[32,640]{1,0:T(8,128)}, f32[32,640]{1,0:T(8,128)S(1)}, u32[]{:S(2)}, u32[]{:S(2)}) collective-permute-start(f32[32,640]{1,0:T(8,128)} %get-tuple-element.24), channel_id=1, source_target_pairs={{0,3},{1,2},{2,1},{3,0},{4,7},{5,6},{6,5},{7,4},{8,11},{9,10},{10,... | collective-permute-start | bytes 245768 | tf_op jit(solution)/shard_map/ppermute | solution.py:469
  38.8 1.7 %collective-permute-start.14 = (f32[32,640]{1,0:T(8,128)}, f32[32,640]{1,0:T(8,128)S(1)}, u32[]{:S(2)}, u32[]{:S(2)}) collective-permute-start(f32[32,640]{1,0:T(8,128)} %get-tuple-element.26), channel_id=1, source_target_pairs={{0,1},{1,0},{2,3},{3,2},{4,5},{5,4},{6,7},{7,6},{8,9},{9,8},{10,11... | collective-permute-start | bytes 245768 | tf_op jit(solution)/shard_map/ppermute | solution.py:469
  40.4 2.2 %collective-permute-done.12.p1 = f32[32,640]{1,0:T(8,128)S(1)} collective-permute-done((f32[32,640]{1,0:T(8,128)}, f32[32,640]{1,0:T(8,128)S(1)}, u32[]{:S(2)}, u32[]{:S(2)}) %collective-permute-start.12) | collective-permute-done | bytes 81952 | tf_op jit(solution)/shard_map/ppermute | solution.py:469
  42.7 5.0 %collective-permute-done.13.p2 = f32[32,640]{1,0:T(8,128)S(1)} collective-permute-done((f32[32,640]{1,0:T(8,128)}, f32[32,640]{1,0:T(8,128)S(1)}, u32[]{:S(2)}, u32[]{:S(2)}) %collective-permute-start.13) | collective-permute-done | bytes 81952 | tf_op jit(solution)/shard_map/ppermute | solution.py:469
  47.7 0.6 %copy-done.13 = f32[32,640]{1,0:T(8,128)} copy-done((f32[32,640]{1,0:T(8,128)}, f32[32,640]{1,0:T(8,128)S(1)}, u32[]{:S(2)}) %copy-start.13) | copy-done | bytes 81944
  48.3 0.0 copy-done.14
  48.3 1.9 %unpack.1 = f32[2,4,4,2,296]{4,3,2,1,0:T(2,128)} custom-call(s32[4,2,4]{2,1,0:T(2,128)} %bitcast.18, f32[32,640]{1,0:T(8,128)} %get-tuple-element.23.p0, f32[32,640]{1,0:T(8,128)} %copy-done.12, f32[32,640]{1,0:T(8,128)} %copy-done.13, f32[32,640]{1,0:T(8,128)} %copy-done.14), custom_call_target="tpu_custom_call" | custom-call | tf_op jit(solution)/shard_map/unpack/pallas_call | solution.py:156
  (37 shorter events, 0.1 us)
Async XLA Ops:
  2.6 9.2 %collective-permute-start.2 = (f32[32,640]{1,0:T(8,128)}, f32[32,640]{1,0:T(8,128)S(1)}, u32[]{:S(2)}, u32[]{:S(2)}) collective-permute-start(f32[32,640]{1,0:T(8,128)} %get-tuple-element.16.c0), channel_id=1, source_target_pairs={{0,3},{1,2},{2,1},{3,0},{4,7},{5,6},{6,5},{7,4},{8,11},{9,10},{10,... | collective-permute-start | bytes 245768 | tf_op jit(solution)/shard_map/ppermute | solution.py:469
  7.7 7.1 %collective-permute-start.1 = (f32[32,640]{1,0:T(8,128)}, f32[32,640]{1,0:T(8,128)S(1)}, u32[]{:S(2)}, u32[]{:S(2)}) collective-permute-start(f32[32,640]{1,0:T(8,128)} %get-tuple-element.16.c0), channel_id=1, source_target_pairs={{0,2},{1,3},{2,0},{3,1},{4,6},{5,7},{6,4},{7,5},{8,10},{9,11},{10,... | collective-permute-start | bytes 245768 | tf_op jit(solution)/shard_map/ppermute | solution.py:469
  7.7 8.6 %collective-permute-start = (f32[32,640]{1,0:T(8,128)}, f32[32,640]{1,0:T(8,128)S(1)}, u32[]{:S(2)}, u32[]{:S(2)}) collective-permute-start(f32[32,640]{1,0:T(8,128)} %get-tuple-element.16.c0), channel_id=1, source_target_pairs={{0,1},{1,0},{2,3},{3,2},{4,5},{5,4},{6,7},{7,6},{8,9},{9,8},{10,11... | collective-permute-start | bytes 245768 | tf_op jit(solution)/shard_map/ppermute | solution.py:469
  8.3 8.1 %collective-permute-start.8 = (f32[240,128]{1,0:T(8,128)}, f32[240,128]{1,0:T(8,128)S(1)}, u32[]{:S(2)}, u32[]{:S(2)}) collective-permute-start(f32[240,128]{1,0:T(8,128)} %get-tuple-element.18.refs_0_), channel_id=1, source_target_pairs={{0,4},{4,0},{8,12},{12,8},{16,20},{20,16},{24,28},{28,24},{1,5},{5... | collective-permute-start | bytes 368648 | tf_op jit(solution)/shard_map/ppermute | solution.py:469
  8.4 8.8 %collective-permute-start.7 = (f32[240,128]{1,0:T(8,128)}, f32[240,128]{1,0:T(8,128)S(1)}, u32[]{:S(2)}, u32[]{:S(2)}) collective-permute-start(f32[240,128]{1,0:T(8,128)} %get-tuple-element.18.refs_0_), channel_id=1, source_target_pairs={{0,24},{4,28},{8,16},{12,20},{16,8},{20,12},{24,0},{28,4},{1,25},{... | collective-permute-start | bytes 368648 | tf_op jit(solution)/shard_map/ppermute | solution.py:469
  11.8 10.0 %copy-start = (f32[32,640]{1,0:T(8,128)}, f32[32,640]{1,0:T(8,128)S(1)}, u32[]{:S(2)}) copy-start(f32[32,640]{1,0:T(8,128)S(1)} %collective-permute-done.2.c3) | copy-start | bytes 245764
  11.8 6.1 %collective-permute-start.6 = (f32[240,128]{1,0:T(8,128)}, f32[240,128]{1,0:T(8,128)S(1)}, u32[]{:S(2)}, u32[]{:S(2)}) collective-permute-start(f32[240,128]{1,0:T(8,128)} %get-tuple-element.18.refs_0_), channel_id=1, source_target_pairs={{0,16},{4,20},{8,24},{12,28},{16,0},{20,4},{24,8},{28,12},{1,17},{... | collective-permute-start | bytes 368648 | tf_op jit(solution)/shard_map/ppermute | solution.py:469
  14.8 7.0 %copy-start.1 = (f32[32,640]{1,0:T(8,128)}, f32[32,640]{1,0:T(8,128)S(1)}, u32[]{:S(2)}) copy-start(f32[32,640]{1,0:T(8,128)S(1)} %collective-permute-done.1.c2) | copy-start | bytes 245764
  14.8 5.1 %collective-permute-start.5 = (f32[240,128]{1,0:T(8,128)}, f32[240,128]{1,0:T(8,128)S(1)}, u32[]{:S(2)}, u32[]{:S(2)}) collective-permute-start(f32[240,128]{1,0:T(8,128)} %get-tuple-element.18.refs_0_), channel_id=1, source_target_pairs={{0,8},{4,12},{8,0},{12,4},{16,24},{20,28},{24,16},{28,20},{1,9},{5... | collective-permute-start | bytes 368648 | tf_op jit(solution)/shard_map/ppermute | solution.py:469
  16.3 5.5 %copy-start.2 = (f32[32,640]{1,0:T(8,128)}, f32[32,640]{1,0:T(8,128)S(1)}, u32[]{:S(2)}) copy-start(f32[32,640]{1,0:T(8,128)S(1)} %collective-permute-done.c1) | copy-start | bytes 245764
  16.3 5.4 %collective-permute-start.3 = (f32[64,640]{1,0:T(8,128)S(1)}, f32[64,640]{1,0:T(8,128)S(1)}, u32[]{:S(2)}, u32[]{:S(2)}) collective-permute-start(f32[64,640]{1,0:T(8,128)S(1)} %maximum_bitcast_fusion), channel_id=1, source_target_pairs={{0,4},{4,0},{8,12},{12,8},{16,20},{20,16},{24,28},{28,24},{1,5},{5... | collective-permute-start | bytes 491528 | tf_op jit(solution)/shard_map/ppermute | solution.py:469
  16.5 5.3 %copy-start.5 = (f32[240,128]{1,0:T(8,128)}, f32[240,128]{1,0:T(8,128)S(1)}, u32[]{:S(2)}) copy-start(f32[240,128]{1,0:T(8,128)S(1)} %collective-permute-done.8.refs_4_) | copy-start | bytes 368644
  16.5 5.3 %collective-permute-start.4 = (f32[64,640]{1,0:T(8,128)S(1)}, f32[64,640]{1,0:T(8,128)S(1)}, u32[]{:S(2)}, u32[]{:S(2)}) collective-permute-start(f32[64,640]{1,0:T(8,128)S(1)} %maximum_bitcast_fusion.1), channel_id=1, source_target_pairs={{4,8},{12,16},{20,24},{8,4},{16,12},{24,20},{5,9},{13,17},{21,25},... | collective-permute-start | bytes 491528 | tf_op jit(solution)/shard_map/ppermute | solution.py:486
  17.2 4.6 %copy-start.6 = (f32[240,128]{1,0:T(8,128)}, f32[240,128]{1,0:T(8,128)S(1)}, u32[]{:S(2)}) copy-start(f32[240,128]{1,0:T(8,128)S(1)} %collective-permute-done.7.refs_3_) | copy-start | bytes 368644
  17.8 4.0 %copy-start.7 = (f32[240,128]{1,0:T(8,128)}, f32[240,128]{1,0:T(8,128)S(1)}, u32[]{:S(2)}) copy-start(f32[240,128]{1,0:T(8,128)S(1)} %collective-permute-done.6.refs_2_) | copy-start | bytes 368644
  19.9 1.9 %copy-start.8 = (f32[240,128]{1,0:T(8,128)}, f32[240,128]{1,0:T(8,128)S(1)}, u32[]{:S(2)}) copy-start(f32[240,128]{1,0:T(8,128)S(1)} %collective-permute-done.5.refs_1_) | copy-start | bytes 368644
  19.9 1.3 %collective-permute-start.9 = (f32[240,128]{1,0:T(8,128)S(1)}, f32[240,128]{1,0:T(8,128)S(1)}, u32[]{:S(2)}, u32[]{:S(2)}) collective-permute-start(f32[240,128]{1,0:T(8,128)S(1)} %collective-permute-done.5.refs_1_), channel_id=1, source_target_pairs={{0,4},{4,0},{8,12},{12,8},{16,20},{20,16},{24,28},{28,24},{1,5},{5... | collective-permute-start | bytes 368648 | tf_op jit(solution)/shard_map/ppermute | solution.py:469
  19.9 1.5 %collective-permute-start.10 = (f32[240,128]{1,0:T(8,128)S(1)}, f32[240,128]{1,0:T(8,128)S(1)}, u32[]{:S(2)}, u32[]{:S(2)}) collective-permute-start(f32[240,128]{1,0:T(8,128)S(1)} %collective-permute-done.6.refs_2_), channel_id=1, source_target_pairs={{0,4},{4,0},{8,12},{12,8},{16,20},{20,16},{24,28},{28,24},{1,5},{5... | collective-permute-start | bytes 368648 | tf_op jit(solution)/shard_map/ppermute | solution.py:469
  20.4 1.3 %collective-permute-start.11 = (f32[240,128]{1,0:T(8,128)S(1)}, f32[240,128]{1,0:T(8,128)S(1)}, u32[]{:S(2)}, u32[]{:S(2)}) collective-permute-start(f32[240,128]{1,0:T(8,128)S(1)} %collective-permute-done.7.refs_3_), channel_id=1, source_target_pairs={{0,4},{4,0},{8,12},{12,8},{16,20},{20,16},{24,28},{28,24},{1,5},{5... | collective-permute-start | bytes 368648 | tf_op jit(solution)/shard_map/ppermute | solution.py:469
  21.2 0.6 %copy-start.9 = (f32[240,128]{1,0:T(8,128)}, f32[240,128]{1,0:T(8,128)S(1)}, u32[]{:S(2)}) copy-start(f32[240,128]{1,0:T(8,128)S(1)} %collective-permute-done.9.refs_5_) | copy-start | bytes 368644
  21.4 0.7 %copy-start.10 = (f32[240,128]{1,0:T(8,128)}, f32[240,128]{1,0:T(8,128)S(1)}, u32[]{:S(2)}) copy-start(f32[240,128]{1,0:T(8,128)S(1)} %collective-permute-done.10.refs_6_) | copy-start | bytes 368644
  21.7 0.6 %copy-start.11 = (f32[240,128]{1,0:T(8,128)}, f32[240,128]{1,0:T(8,128)S(1)}, u32[]{:S(2)}) copy-start(f32[240,128]{1,0:T(8,128)S(1)} %collective-permute-done.11.refs_7_) | copy-start | bytes 368644
  21.7 0.7 %copy-start.3 = (f32[64,640]{1,0:T(8,128)}, f32[64,640]{1,0:T(8,128)S(1)}, u32[]{:S(2)}) copy-start(f32[64,640]{1,0:T(8,128)S(1)} %collective-permute-done.3.inner_ref) | copy-start | bytes 491524
  22.4 0.7 %copy-start.4 = (f32[64,640]{1,0:T(8,128)}, f32[64,640]{1,0:T(8,128)S(1)}, u32[]{:S(2)}) copy-start(f32[64,640]{1,0:T(8,128)S(1)} %collective-permute-done.4.outer_ref) | copy-start | bytes 491524
  36.0 6.7 %collective-permute-start.12 = (f32[32,640]{1,0:T(8,128)}, f32[32,640]{1,0:T(8,128)S(1)}, u32[]{:S(2)}, u32[]{:S(2)}) collective-permute-start(f32[32,640]{1,0:T(8,128)} %get-tuple-element.24), channel_id=1, source_target_pairs={{0,3},{1,2},{2,1},{3,0},{4,7},{5,6},{6,5},{7,4},{8,11},{9,10},{10,... | collective-permute-start | bytes 245768 | tf_op jit(solution)/shard_map/ppermute | solution.py:469
  38.7 8.9 %collective-permute-start.13 = (f32[32,640]{1,0:T(8,128)}, f32[32,640]{1,0:T(8,128)S(1)}, u32[]{:S(2)}, u32[]{:S(2)}) collective-permute-start(f32[32,640]{1,0:T(8,128)} %get-tuple-element.25), channel_id=1, source_target_pairs={{0,2},{1,3},{2,0},{3,1},{4,6},{5,7},{6,4},{7,5},{8,10},{9,11},{10,... | collective-permute-start | bytes 245768 | tf_op jit(solution)/shard_map/ppermute | solution.py:469
  38.8 8.9 %collective-permute-start.14 = (f32[32,640]{1,0:T(8,128)}, f32[32,640]{1,0:T(8,128)S(1)}, u32[]{:S(2)}, u32[]{:S(2)}) collective-permute-start(f32[32,640]{1,0:T(8,128)} %get-tuple-element.26), channel_id=1, source_target_pairs={{0,1},{1,0},{2,3},{3,2},{4,5},{5,4},{6,7},{7,6},{8,9},{9,8},{10,11... | collective-permute-start | bytes 245768 | tf_op jit(solution)/shard_map/ppermute | solution.py:469
  42.7 5.0 %copy-start.12 = (f32[32,640]{1,0:T(8,128)}, f32[32,640]{1,0:T(8,128)S(1)}, u32[]{:S(2)}) copy-start(f32[32,640]{1,0:T(8,128)S(1)} %collective-permute-done.12.p1) | copy-start | bytes 245764
  47.7 0.6 %copy-start.13 = (f32[32,640]{1,0:T(8,128)}, f32[32,640]{1,0:T(8,128)S(1)}, u32[]{:S(2)}) copy-start(f32[32,640]{1,0:T(8,128)S(1)} %collective-permute-done.13.p2) | copy-start | bytes 245764
  47.7 0.6 %copy-start.14 = (f32[32,640]{1,0:T(8,128)}, f32[32,640]{1,0:T(8,128)S(1)}, u32[]{:S(2)}) copy-start(f32[32,640]{1,0:T(8,128)S(1)} %collective-permute-done.14.p3) | copy-start | bytes 245764
